TPU v7x, 32 devices: a whole 2x2x4 slice. The times are simulated.
32 devices in a mesh: ty: 4 (over y, core), tx: 8 (over z, x).
Axes of the slice: x: 2, y: 2, z: 4, core: 2. Of those that a mesh axis runs over, the one named last changes fastest.
Arguments:
- source_fields: float32 [8, 384, 2048], P(None, 'ty', 'tx'), may hold values from -6 to 6
- diffusivity: float32 [384, 2048], P('ty', 'tx'), may hold values from 0.03 to 0.24
- cell_area: float32 [384, 2048], P('ty', 'tx'), may hold values from 0.5 to 2
- pair_block: int32 [8192], P(('ty', 'tx')), may hold values from 0 to 191
- pair_owner: int32 [8192, 1], P(('ty', 'tx')), may hold values from 0 to 31; in each aligned block of 256 rows (0 to 255, 256 to 511, ...) at most 16 rows name the same one
- pair_target: int32 [8192], P(('ty', 'tx')), may hold values from 0 to 15
- weight_blocks: bfloat16 [8192, 128, 128], P(('ty', 'tx')), may hold values from 0.0099487305 to 0.099609375
- target_area: float32 [512, 128], P(('ty', 'tx')), may hold values from 1 to 4
Outputs:
- regridded: float32 [512, 8, 128], P(('ty', 'tx'))
Inputs may be any that keep to these rules, and one draw needn't show every extreme that they name: `pair_owner`: among the 256 pairs held by one device, no owner is named more than 16 times; some device names some owner exactly 16 times.
All inputs are finite; a program needn't handle non-finite values.
Results may differ from a plain program's by a relative error of at most 0.0018.
Values sent between devices are 32-bit elements; how exact they have to be, the bound alone decides.
No kernel may reach another device: no remote copies, remote signals or barrier semaphores. Data moves between devices by JAX's collectives and lax.ppermute only.
A program may use at most 64 MiB of HBM per device.

v0:
```python
import functools

import jax
import jax.numpy as jnp
from jax import lax
from jax.experimental import pallas as pl
from jax.experimental.pallas import tpu as pltpu
from jax.sharding import PartitionSpec as P

BH = 8
BW = 16
LANES = 128
SUB = 8
HALO = 2
EDGE = 4
BATCH = 32
KINDS = 4
LAG = 3
VMEM = pl.BlockSpec(memory_space=pltpu.VMEM)
HBM = pl.BlockSpec(memory_space=pltpu.HBM)


def run_copies(copies):
    for copy in copies:
        copy.start()
    for copy in copies:
        copy.wait()


def rounded(values):
    return values.astype(jnp.bfloat16).astype(jnp.float32)


def pack_kernel(
    rows, fields_hbm, rates_hbm, area_hbm,
    west_cols, east_cols, first_rows, last_rows, own_cols, narrow, rates, area, sems,
):
    width = rates.shape[1]
    parts, count = narrow.shape[:2]
    copies = [
        pltpu.make_async_copy(
            fields_hbm.at[:, :, pl.ds(h * LANES, LANES)], narrow.at[h, :, pl.ds(0, rows)], sems.at[2 + h]
        )
        for h in range(parts)
    ]
    copies.append(pltpu.make_async_copy(rates_hbm, rates, sems.at[0]))
    copies.append(pltpu.make_async_copy(area_hbm, area, sems.at[1]))
    run_copies(copies)
    for out, start in ((first_rows, 0), (last_rows, rows - HALO)):
        for r in range(HALO):
            for h in range(parts):
                for v in range(count):
                    line = narrow[h, v, start + r : start + r + 1, :]
                    out[r * 16 + v : r * 16 + v + 1, h * LANES : (h + 1) * LANES] = line
            out[r * 16 + SUB : r * 16 + 16, :] = jnp.broadcast_to(rates[start + r : start + r + 1, :], (SUB, width))
    pad = jnp.zeros((LANES - rows, LANES), jnp.float32)
    left = lax.broadcasted_iota(jnp.int32, (rows, LANES), 1) < LANES // 2
    for v in range(count + 1):
        if v == count:
            west, east, high = rates[:, :LANES], rates[:, width - LANES :], SUB
        else:
            west, east, high = narrow[0, v, :rows, :], narrow[parts - 1, v, :rows, :], 1
        sides = jnp.concatenate([jnp.where(left, west, east), pad], axis=0).T
        for c in range(EDGE):
            for side, line in ((0, sides[c : c + 1, :]), (1, sides[LANES - EDGE + c : LANES - EDGE + c + 1, :])):
                line = jnp.broadcast_to(line, (high, LANES))
                at = (side * EDGE + c) * 16 + v
                own_cols[at : at + high, :] = line
    for out, first in ((west_cols, 0), (east_cols, 2 * EDGE - HALO)):
        lines = [own_cols[(first + c) * 16 : (first + c) * 16 + SUB, :] for c in range(HALO)]
        lines += [own_cols[(first + c) * 16 + SUB : (first + c) * 16 + SUB + 1, :] for c in range(HALO)]
        out[...] = jnp.concatenate(lines + [jnp.zeros((SUB - HALO, LANES), jnp.float32)], axis=0)


def came_column(cols, c):
    rate = cols[HALO * SUB + c : HALO * SUB + c + 1, :]
    return cols[c * SUB : (c + 1) * SUB, :], jnp.broadcast_to(rate, (SUB, LANES))


def corner_kernel(rows, west, east, first_rows, last_rows, _, rows_even, rows_odd):
    width = first_rows.shape[1]
    lane = lax.broadcasted_iota(jnp.int32, (16, LANES), 1)

    near_east = jnp.concatenate(came_column(east, 0), axis=0)
    near_west = jnp.concatenate(came_column(west, HALO - 1), axis=0)

    def beyond(y):
        tile = jnp.where(lane == 0, pltpu.roll(near_east, -y % LANES, 1), 0.0)
        return jnp.where(lane == LANES - 1, pltpu.roll(near_west, (LANES - 1 - y) % LANES, 1), tile)

    first = packed_rows(first_rows, beyond(0))
    last = packed_rows(last_rows, beyond(rows - 1))
    even = lax.axis_index("ty") & 1 == 0
    rows_even[...] = jnp.where(even, last, first)
    rows_odd[...] = jnp.where(even, first, last)


def packed_rows(lines, beyond):
    width = lines.shape[1]
    parts = width // LANES
    rates = [lines[r * 16 + SUB : r * 16 + SUB + 1, h * LANES : (h + 1) * LANES] for r in range(HALO) for h in range(parts)]
    rates.append(beyond[SUB : SUB + 1, :])
    rates.append(jnp.zeros((SUB - len(rates), LANES), jnp.float32))
    below = [beyond[:SUB, :], jnp.concatenate(rates, axis=0)] + [jnp.zeros((SUB, LANES), jnp.float32)] * (parts - 2)
    return jnp.concatenate([lines[:SUB, :], lines[16 : 16 + SUB, :], jnp.concatenate(below, axis=1)], axis=0)


def unpacked_rows(lines):
    parts = lines.shape[1] // LANES

    def rate(at):
        return jnp.broadcast_to(lines[HALO * SUB + at : HALO * SUB + at + 1, LANES : 2 * LANES], (SUB, LANES))

    rows = [
        (lines[r * SUB : (r + 1) * SUB, :], jnp.concatenate([rate(r * parts + h) for h in range(parts)], axis=1))
        for r in range(HALO)
    ]
    return rows, (lines[HALO * SUB :, :LANES], rate(HALO * parts))


def swap_granules(tiles, chunk):
    for step in (4, 2, 1):
        upper = (chunk & step) != 0
        swapped = list(tiles)
        for i in range(8):
            if i & step == 0:
                a, b = tiles[i], tiles[i + step]
                swapped[i] = jnp.where(upper, pltpu.roll(b, step * BW, 1), a)
                swapped[i + step] = jnp.where(upper, b, pltpu.roll(a, LANES - step * BW, 1))
        tiles = swapped
    return tiles


def stage_masks(n_ty, n_tx):
    x, y, z, far = 1, 2 * n_tx, 2, 4
    others = [1 << i for i in range(3, n_tx.bit_length() - 1)] + [n_tx << i for i in range(2, n_ty.bit_length() - 1)]
    others = [[i] for i in others]
    return [[x], [y, z], [far]] + others, [[y], [z, x], [far]] + others


def target_rows(block, owner, target, sizes):
    n_ty, n_tx, targets, block_rows, block_columns = sizes
    relative = owner ^ (lax.axis_index("ty") * n_tx + lax.axis_index("tx"))

    def bit(value, mask):
        return lax.shift_right_logical(value, mask.bit_length() - 1) & 1

    row = jnp.zeros_like(owner)
    core = bit(owner, n_tx)
    for mask_0, mask_1 in zip(*(sum(stages, []) for stages in stage_masks(n_ty, n_tx))):
        row = row * 2 + jnp.where(core == 0, bit(relative, mask_0), bit(relative, mask_1))
    at_edge = (block < block_columns) | (block >= (block_rows - 1) * block_columns)
    row = row * targets + target
    kept = (row < n_ty * n_tx * targets // 4).astype(jnp.int32)
    return row, jnp.where(bit(relative, n_tx) == 1, at_edge.astype(jnp.int32), 2 + kept)


def pair_bits(blocks, pairs):
    return (blocks - 1).bit_length(), (pairs - 1).bit_length()


def pair_table(block, row, kind, row_count, widths):
    lines = kind.shape[0]
    count = lines * LANES

    def rows_of(x):
        return [x[i : i + 1, :].astype(jnp.float32) for i in range(lines)]

    def columns_of(rows):
        return [jnp.broadcast_to(row, (LANES, LANES)).T for row in rows]

    number = lax.broadcasted_iota(jnp.int32, kind.shape, 0) * LANES + lax.broadcasted_iota(jnp.int32, kind.shape, 1)
    keys = rows_of((kind * row_count + row) * count + number)
    key_columns = columns_of(keys)
    places = [sum(jnp.sum((c < row).astype(jnp.float32), axis=0, keepdims=True) for c in key_columns) for row in keys]
    lane = lax.broadcasted_iota(jnp.int32, (1, LANES), 1)
    counts, below = jnp.zeros((1, LANES), jnp.float32), jnp.zeros((1, 1), jnp.float32)
    for k in range(KINDS):
        of_kind = [(x == k) for x in rows_of(kind)]
        places = [jnp.where(m, p + (k * count - below), p) for m, p in zip(of_kind, places)]
        number_of = sum(jnp.sum(m.astype(jnp.float32), axis=1, keepdims=True) for m in of_kind)
        counts = jnp.where(lane == k, number_of, counts)
        below = below + number_of
    lanes = lax.broadcasted_iota(jnp.int32, (LANES, KINDS * count), 1).astype(jnp.float32)
    total = jnp.zeros((16, KINDS * count), jnp.float32)
    for i, column in enumerate(columns_of(places)):
        hot = (jnp.concatenate([column] * (KINDS * lines), axis=1) == lanes).astype(jnp.float32).astype(jnp.bfloat16)
        stack = [part[i : i + 1, :] for x in (block, number, row) for part in (x & 255, lax.shift_right_logical(x, 8))]
        stack = jnp.concatenate([x.astype(jnp.float32) for x in stack], axis=0)
        stack = jnp.concatenate([stack, jnp.zeros((16 - stack.shape[0], LANES), jnp.float32)], axis=0)
        total = total + jnp.dot(stack.astype(jnp.bfloat16), hot, preferred_element_type=jnp.float32)
    fields = [total[2 * f : 2 * f + 1, :].astype(jnp.int32) + 256 * total[2 * f + 1 : 2 * f + 2, :].astype(jnp.int32) for f in range(3)]
    words = fields[0] + (fields[1] << widths[0]) + (fields[2] << sum(widths))
    return [words[:, o * LANES : (o + 1) * LANES] for o in range(KINDS * lines)] + [counts.astype(jnp.int32)]


def smooth_kernel(
    rows, sizes, narrow, rates, area, pairs_hbm, owner_hbm, target_hbm, weights,
    blocks, own_rows, area_cols, table, held,
    once, scaled, face_e, face_n, pairs, owner, target, sems,
):
    width = rates.shape[1]
    count = blocks.shape[1]
    parts = width // LANES
    pitch = narrow.shape[0] // (parts * count)
    lines = owner.shape[0]
    copies = [
        pltpu.make_async_copy(pairs_hbm, pairs, sems.at[0]),
        pltpu.make_async_copy(owner_hbm, owner, sems.at[1]),
        pltpu.make_async_copy(target_hbm, target, sems.at[2]),
    ]
    for copy in copies:
        copy.start()
    load = pltpu.make_async_copy(weights, held, sems.at[3])
    load.start()
    own = rates[...]
    face_e[...] = 0.5 * (own + pltpu.roll(own, width - 1, 1))
    face_n[...] = 0.5 * (own + pltpu.roll(own, rows - 1, 0))
    pad = jnp.zeros((LANES - rows, LANES), jnp.float32)
    left = lax.broadcasted_iota(jnp.int32, (rows, LANES), 1) < LANES // 2
    sides = jnp.concatenate([jnp.where(left, area[:, :LANES], area[:, width - LANES :]), pad], axis=0).T
    for c in range(HALO):
        area_cols[c * SUB : (c + 1) * SUB, :] = jnp.broadcast_to(sides[c : c + 1, :], (SUB, LANES))
        line = sides[LANES - HALO + c : LANES - HALO + c + 1, :]
        area_cols[(HALO + c) * SUB : (HALO + c + 1) * SUB, :] = jnp.broadcast_to(line, (SUB, LANES))

    def row_of(y):
        return jnp.concatenate(
            [narrow[pl.ds(h * count * pitch + y, count, stride=pitch), :] for h in range(parts)], axis=1
        )

    for r in range(EDGE):
        own_rows[r] = row_of(r)
        own_rows[EDGE + r] = row_of(rows - EDGE + r)

    def step(v, v_n, y, below):
        k_e = jnp.broadcast_to(face_e[pl.ds(y, 1), :], v.shape)
        k_n = jnp.broadcast_to(face_n[pl.ds(y, 1), :], v.shape)
        to_east = k_e * (pltpu.roll(v, width - 1, 1) - v)
        to_north = k_n * (v_n - v)
        return v + to_east - pltpu.roll(to_east, 1, 1) + to_north - below, to_north

    chunk = lax.broadcasted_iota(jnp.int32, (SUB, LANES), 1) // BW
    columns = width // BW
    groups = rows // BH

    def group(i, carry):
        below_1, below_2 = carry
        third = jnp.maximum(i - 3, 0)
        for h in range(parts):
            tiles = swap_granules([scaled[j, :, h * LANES : (h + 1) * LANES] for j in range(BH)], chunk)
            for c, tile in enumerate(tiles):
                blocks[third * columns + h * 8 + c] = tile
        second = jnp.clip(i - 2, 0, groups - 1)
        out = []
        for j in range(BH):
            y = second * BH + j
            smooth, below_2 = step(once[y], once[y + 1], y, below_2)
            out.append(rounded(jnp.broadcast_to(area[pl.ds(y, 1), :], smooth.shape) * smooth))
        fresh = []
        first = jnp.minimum(i, groups - 1) * BH
        lines = [row_of(first + j) for j in range(BH + 1)]
        for j in range(BH):
            smooth, below_1 = step(lines[j], lines[j + 1], first + j, below_1)
            fresh.append(smooth)
        for j in range(BH):
            scaled[j] = out[j]
        for j in range(BH):
            once[i * BH + j] = fresh[j]
        return below_1, below_2

    zero = jnp.zeros((count, width), jnp.float32)
    lax.fori_loop(0, groups + LAG, group, (zero, zero))

    for copy in copies:
        copy.wait()
    block = pairs[...]
    row_count = sizes[0] * sizes[1] * sizes[2] // 2
    row, kind = target_rows(block, owner[...], target[...], sizes)
    for i, line in enumerate(pair_table(block, row, kind, row_count, pair_bits(blocks.shape[0], held.shape[0]))):
        table[i : i + 1, :] = line
    load.wait()


def add_products(table, blocks, held, sums, kind, batch, first_row=0):
    lines = held.shape[0] // LANES
    for_block, for_pair = pair_bits(blocks.shape[0], held.shape[0])
    number_of = table[KINDS * lines, kind]
    per_line = LANES // batch

    def products(g, carry):
        line = kind * lines + lax.shift_right_logical(g, per_line.bit_length() - 1)
        start = (g & (per_line - 1)) * batch
        words = [table[line, start + j] for j in range(batch)]
        results = []
        for one, two in zip(words[::2], words[1::2]):
            first, second = [blocks[word & ((1 << for_block) - 1)] for word in (one, two)]
            nothing = jnp.zeros_like(first)
            both = jnp.concatenate(
                [jnp.concatenate([first, nothing], axis=1), jnp.concatenate([nothing, second], axis=1)], axis=0
            ).astype(jnp.bfloat16)
            weights = [held[lax.shift_right_logical(word, for_block) & ((1 << for_pair) - 1)] for word in (one, two)]
            product = jnp.dot(both, jnp.concatenate(weights, axis=0), preferred_element_type=jnp.float32)
            results += [product[:SUB, :], product[SUB:, :]]
        left = number_of - g * batch
        total, row = carry
        rows = [lax.shift_right_logical(word, for_block + for_pair) - first_row for word in words]
        rows = [jnp.where(j < left, new, rows[0]) for j, new in enumerate(rows)]
        old = [sums[new] for new in rows]
        for j, result in enumerate(results):
            real = j < left
            new = jnp.where(real, rows[j], row)
            total = jnp.where(new == row, total, old[j]) + jnp.where(real, result, 0.0)
            row = new
            sums[row] = total
        return total, row

    start = (jnp.zeros(sums.shape[1:], jnp.float32), jnp.int32(-1))
    lax.fori_loop(0, lax.div(number_of + batch - 1, batch), products, start)


def clear(sums):
    def rows(i, carry):
        sums[pl.ds(i * SUB, SUB)] = jnp.zeros((SUB,) + sums.shape[1:], jnp.float32)
        return carry

    lax.fori_loop(0, sums.shape[0] // SUB, rows, 0)


def sum_kernel(kind, first_row, table_vmem, blocks, held, sums, table, sem):
    copy = pltpu.make_async_copy(table_vmem, table, sem)
    copy.start()
    clear(sums)
    copy.wait()
    add_products(table, blocks, held, sums, kind, BATCH, first_row)


def split(ref, c):
    return ref[c * 16 : c * 16 + SUB, :], ref[c * 16 + SUB : c * 16 + 16, :]


def smoothed_columns(v, r):
    to_east = [0.5 * (r[i] + r[i + 1]) * (v[i + 1] - v[i]) for i in range(len(v) - 1)]
    out = []
    for i in range(1, len(v) - 1):
        k_n = 0.5 * (r[i] + pltpu.roll(r[i], LANES - 1, 1))
        to_north = k_n * (pltpu.roll(v[i], LANES - 1, 1) - v[i])
        out.append(v[i] + to_east[i] - to_east[i - 1] + to_north - pltpu.roll(to_north, 1, 1))
    return out


def inner_kernel(
    rows, columns, east, west, table_vmem, own_cols, area_cols, held, blocks_in, sums, blocks, table, sem
):
    copy = pltpu.make_async_copy(table_vmem, table, sem)
    copy.start()
    clear(sums)
    lane = lax.broadcasted_iota(jnp.int32, (SUB, LANES), 1)
    halves = (
        ([came_column(west, c) for c in range(HALO)] + [split(own_cols, c) for c in range(EDGE)], 0, 0),
        ([split(own_cols, EDGE + c) for c in range(EDGE)] + [came_column(east, c) for c in range(HALO)], columns - 1, BW - HALO),
    )
    for side, (lines, column, granule_start) in enumerate(halves):
        v, r = [x for x, _ in lines], [x for _, x in lines]
        twice = smoothed_columns(smoothed_columns(v, r), r[1:-1])
        fixed = []
        for c in range(HALO):
            at = (side * HALO + c) * SUB
            fixed.append(rounded(area_cols[at : at + SUB, :] * twice[c]))
        for i in range(rows // BH):
            tile = blocks_in[i * columns + column]
            for c in range(HALO):
                spread = jnp.take_along_axis(fixed[c], i * BH + lane // BW, axis=1)
                tile = jnp.where(lane % BW == granule_start + c, spread, tile)
            blocks[i * columns + column] = tile
    copy.wait()
    add_products(table, blocks, held, sums, 0, BATCH)


def edge_kernel(
    rows, n_ty, rows_odd, rows_even, table_vmem, rates, area, own_rows, east, west, held,
    sums_in, blocks_in, sums, blocks, table, sem,
):
    width = rates.shape[1]
    parts = width // LANES
    columns = width // BW
    count = sums.shape[1]
    copy = pltpu.make_async_copy(table_vmem, table, sem)
    copy.start()
    lane = lax.broadcasted_iota(jnp.int32, (SUB, LANES), 1)

    even = lax.axis_index("ty") & 1 == 0
    south, beyond_south = unpacked_rows(jnp.where(even, rows_odd[...], rows_even[...]))
    north, beyond_north = unpacked_rows(jnp.where(even, rows_even[...], rows_odd[...]))

    def beyond(part, y):
        if y < 0 or y >= rows:
            return (beyond_south if y < 0 else beyond_north)[part]
        e_0, e_1 = came_column(east, 0)[part], came_column(east, 1)[part]
        w_0, w_1 = came_column(west, 0)[part], came_column(west, 1)[part]
        tile = jnp.where(lane == 0, pltpu.roll(e_0, -y % LANES, 1), 0.0)
        tile = jnp.where(lane == 1, pltpu.roll(e_1, (1 - y) % LANES, 1), tile)
        tile = jnp.where(lane == LANES - 2, pltpu.roll(w_0, (LANES - 2 - y) % LANES, 1), tile)
        return jnp.where(lane == LANES - 1, pltpu.roll(w_1, (LANES - 1 - y) % LANES, 1), tile)

    wide = width + LANES
    nothing = jnp.zeros((SUB, LANES), jnp.float32)

    def own_row(y):
        at = y if y < EDGE else EDGE + y - (rows - EDGE)
        rate = jnp.broadcast_to(rates[y : y + 1, :], (SUB, width))
        return own_rows[at], rate

    def smoothed_rows(v, r, shut):
        k_n = [0.5 * (r[i] + r[i + 1]) for i in range(len(v) - 1)]
        at, closed = shut
        k_n[at] = jnp.where(closed, 0.0, k_n[at])
        to_north = [k_n[i] * (v[i + 1] - v[i]) for i in range(len(v) - 1)]
        out = []
        for i in range(1, len(v) - 1):
            k_e = 0.5 * (r[i] + pltpu.roll(r[i], wide - 1, 1))
            to_east = k_e * (pltpu.roll(v[i], wide - 1, 1) - v[i])
            out.append(v[i] + to_east - pltpu.roll(to_east, 1, 1) + to_north[i] - to_north[i - 1])
        return out

    my_ty = lax.axis_index("ty")
    for start, closed_at, closed in ((-HALO, 1, my_ty == 0), (rows - EDGE, 3, my_ty == n_ty - 1)):
        v, r = [], []
        for i in range(HALO + EDGE):
            y = start + i
            if y < 0:
                value, rate = south[y + HALO]
            elif y >= rows:
                value, rate = north[y - rows]
            else:
                value, rate = own_row(y)
            near = -1 <= y <= rows
            v.append(jnp.concatenate([value, beyond(0, y) if near else nothing], axis=1))
            r.append(jnp.concatenate([rate, beyond(1, y) if near else nothing], axis=1))
        once = smoothed_rows(v, r, (closed_at, closed))
        twice = smoothed_rows(once, r[1:-1], (closed_at - 1, closed))
        first = start + HALO
        lines = [
            rounded(jnp.broadcast_to(area[first + c : first + c + 1, :], (SUB, width)) * twice[c][:, :width])
            for c in range(HALO)
        ]
        block_row, inner = first // BH, first % BH
        for b in range(columns):
            h = b // (LANES // BW)
            at = block_row * columns + b
            tile = blocks_in[at]
            for c in range(HALO):
                moved = pltpu.roll(lines[c][:, h * LANES : (h + 1) * LANES], (inner + c - b) * BW % LANES, 1)
                tile = jnp.where(lane // BW == inner + c, moved, tile)
            blocks[at] = tile

    copy.wait()
    add_products(table, blocks, held, sums, 1, BATCH)


def in_hbm(array):
    return pltpu.with_memory_space_constraint(array, pltpu.HBM)


def bit_swap(axis, mask):
    return [(i, i ^ mask) for i in range(lax.axis_size(axis))]


def pairs_of(axis, start):
    size = lax.axis_size(axis)
    return [(i, (i + (1 if i % 2 == start else -1)) % size) for i in range(size)]


def in_turn(array, *before):
    return lax.optimization_barrier((array, before))[0]


def parts_of(masks):
    return sorted(range(1, 1 << len(masks[0])), key=lambda q: (-q.bit_count(), -q))


def swap_parts(parts, masks):
    n_ty, n_tx = lax.axis_size("ty"), lax.axis_size("tx")

    def partner(i, q):
        return i ^ sum(m for k, m in enumerate(reversed(masks[i // n_tx % 2])) if q >> k & 1)

    return [
        lax.ppermute(part, ("ty", "tx"), [(i, partner(i, q)) for i in range(n_ty * n_tx)])
        for q, part in zip(parts_of(masks), parts)
    ]


def reduce_rows(terms, stages):
    for masks in stages:
        size = terms[0].shape[0] >> len(masks[0])

        def part(q):
            first, *rest = [x[q * size : (q + 1) * size] for x in terms]
            return sum(rest, start=first)

        parts = lax.optimization_barrier([part(q) for q in parts_of(masks)])
        terms = [part(0)] + swap_parts(parts, masks)
    return sum(terms[1:], start=terms[0])


def on_device(
    source_fields,
    diffusivity,
    cell_area,
    pair_block,
    pair_owner,
    pair_target,
    weight_blocks,
    target_area,
):
    count, rows, width = source_fields.shape
    n_ty, n_tx = lax.axis_size("ty"), lax.axis_size("tx")
    pairs = weight_blocks.shape[0]
    targets, cells = target_area.shape
    source_fields = in_hbm(source_fields)
    diffusivity, cell_area, weight_blocks = in_hbm(diffusivity), in_hbm(cell_area), in_hbm(weight_blocks)

    table_lines = pairs // LANES
    parts, pitch = width // LANES, rows + SUB
    sizes = (n_ty, n_tx, targets, rows // BH, width // BW)
    edge_rows = pltpu.VMEM((HALO * 16, width), jnp.float32)
    edge_cols = pltpu.VMEM((HALO * SUB + SUB, LANES), jnp.float32)
    tile = pltpu.VMEM(diffusivity.shape, jnp.float32)
    west_cols, east_cols, first_rows, last_rows, own_cols, narrow, rates, area = pl.pallas_call(
        functools.partial(pack_kernel, rows),
        out_shape=(
            edge_cols,
            edge_cols,
            edge_rows,
            edge_rows,
            pltpu.VMEM((2 * EDGE * 16, LANES), jnp.float32),
            pltpu.VMEM((parts, count, pitch, LANES), jnp.float32),
            tile,
            tile,
        ),
        in_specs=[HBM] * 3,
        out_specs=(VMEM,) * 8,
        scratch_shapes=[pltpu.SemaphoreType.DMA((2 + parts,))],
        compiler_params=pltpu.CompilerParams(vmem_limit_bytes=16 << 20),
        name="pack_edges",
    )(source_fields, diffusivity, cell_area)
    narrow = narrow.reshape(parts * count * pitch, LANES)

    west = lax.ppermute(east_cols, "tx", [(i, (i + 1) % n_tx) for i in range(n_tx)])
    east = lax.ppermute(west_cols, "tx", [((i + 1) % n_tx, i) for i in range(n_tx)])

    blocks_shape = pltpu.VMEM((rows // BH * (width // BW), count, cells), jnp.float32)
    blocks, own_rows, area_cols, table, held = pl.pallas_call(
        functools.partial(smooth_kernel, rows, sizes),
        out_shape=(
            blocks_shape,
            pltpu.VMEM((2 * EDGE, count, width), jnp.float32),
            pltpu.VMEM((2 * HALO * SUB, LANES), jnp.float32),
            pltpu.VMEM((KINDS * table_lines + SUB, LANES), jnp.int32),
            pltpu.VMEM(weight_blocks.shape, jnp.bfloat16),
        ),
        in_specs=[VMEM] * 3 + [HBM] * 4,
        out_specs=(VMEM,) * 5,
        scratch_shapes=[
            pltpu.VMEM((rows + LAG * BH, count, width), jnp.float32),
            pltpu.VMEM((BH, count, width), jnp.float32),
            pltpu.VMEM(diffusivity.shape, jnp.float32),
            pltpu.VMEM(diffusivity.shape, jnp.float32),
            pltpu.VMEM((table_lines, LANES), jnp.int32),
            pltpu.VMEM((table_lines, LANES), jnp.int32),
            pltpu.VMEM((table_lines, LANES), jnp.int32),
            pltpu.SemaphoreType.DMA((4,)),
        ],
        compiler_params=pltpu.CompilerParams(vmem_limit_bytes=16 << 20),
        cost_estimate=pl.CostEstimate(flops=0, bytes_accessed=12 << 20, transcendentals=0),
        name="smooth_inside",
    )(
        narrow, rates, area,
        *(in_hbm(x.reshape(table_lines, LANES)) for x in (pair_block, pair_owner, pair_target)),
        weight_blocks,
    )

    wide_rows = pltpu.VMEM((HALO * SUB + SUB, width), jnp.float32)
    rows_even, rows_odd = pl.pallas_call(
        functools.partial(corner_kernel, rows),
        out_shape=(wide_rows, wide_rows),
        in_specs=[VMEM] * 5,
        out_specs=(VMEM,) * 2,
        compiler_params=pltpu.CompilerParams(vmem_limit_bytes=16 << 20),
        name="join_corners",
    )(west, east, first_rows, last_rows, area_cols)
    rows_odd = lax.ppermute(rows_odd, "ty", pairs_of("ty", 1))
    rows_even = lax.ppermute(rows_even, "ty", pairs_of("ty", 0))

    half = n_ty * n_tx * targets // 2
    smem_table = [pltpu.SMEM(table.shape, jnp.int32), pltpu.SemaphoreType.DMA]

    def sums_of(kind, first_row, row_count, table, blocks, name):
        return pl.pallas_call(
            functools.partial(sum_kernel, kind, first_row),
            out_shape=pltpu.VMEM((row_count, count, cells), jnp.float32),
            in_specs=[VMEM] * 3,
            out_specs=VMEM,
            scratch_shapes=smem_table,
            compiler_params=pltpu.CompilerParams(vmem_limit_bytes=16 << 20),
            cost_estimate=pl.CostEstimate(
                flops=pairs * count * cells * cells, bytes_accessed=pairs * cells * cells, transcendentals=0
            ),
            name=name,
        )(table, blocks, held)

    sums_shape = pltpu.VMEM((half, count, cells), jnp.float32)
    sums, blocks = pl.pallas_call(
        functools.partial(inner_kernel, rows, width // BW),
        out_shape=(sums_shape, blocks_shape),
        in_specs=[VMEM] * 7,
        out_specs=(VMEM, VMEM),
        scratch_shapes=smem_table,
        input_output_aliases={6: 1},
        compiler_params=pltpu.CompilerParams(vmem_limit_bytes=16 << 20),
        cost_estimate=pl.CostEstimate(
            flops=pairs * count * cells * cells, bytes_accessed=pairs * cells * cells, transcendentals=0
        ),
        name="multiply_inside",
    )(east, west, table, own_cols, area_cols, held, blocks)
    sums, blocks = pl.pallas_call(
        functools.partial(edge_kernel, rows, n_ty),
        out_shape=(sums_shape, blocks_shape),
        in_specs=[VMEM] * 11,
        out_specs=(VMEM, VMEM),
        scratch_shapes=smem_table,
        input_output_aliases={9: 0, 10: 1},
        compiler_params=pltpu.CompilerParams(vmem_limit_bytes=16 << 20),
        name="add_edges",
    )(rows_odd, rows_even, table, rates, area, own_rows, east, west, held, sums, blocks)

    cut = half // 2
    got_sent = lax.ppermute(sums[cut:], "ty", bit_swap("ty", 1))
    got_kept = lax.ppermute(sums[:cut], "ty", bit_swap("ty", 1))
    sent = in_turn(sums_of(2, cut, cut, table, blocks, "multiply_sent") + got_sent)
    stages = list(zip(*stage_masks(n_ty, n_tx)))
    came = swap_parts([sent], stages[0])
    kept = sums_of(3, 0, cut, in_turn(table, sent), blocks, "multiply_kept")
    return reduce_rows([kept, got_kept] + came, stages[1:]) / target_area[:, None, :]


def solution(mesh):
    return jax.shard_map(
        on_device,
        mesh=mesh,
        in_specs=(
            P(None, "ty", "tx"),
            P("ty", "tx"),
            P("ty", "tx"),
            P(("ty", "tx")),
            P(("ty", "tx"), None),
            P(("ty", "tx")),
            P(("ty", "tx"), None, None),
            P(("ty", "tx"), None),
        ),
        out_specs=P(("ty", "tx"), None, None),
        check_vma=False,
    )
```

profile of v0, /device:TPU:0, one launch (start us, length us, event | category | flops | bytes accessed | tf_op | source)
XLA Modules:
  0.0 41.3 jit_solution(17794637230003473861)
XLA Ops:
  0.0 1.5 %pack_edges.1 = (f32[24,128]{1,0:T(8,128)S(1)}, f32[24,128]{1,0:T(8,128)S(1)}, f32[32,256]{1,0:T(8,128)S(1)}, f32[32,256]{1,0:T(8,128)S(1)}, f32[128,128]{1,0:T(...) custom-call(f32[8,96,256]{2,1,0:T(8,128)} %fields_hbm.1, ...), custom_call_target="tpu_custom_call" | custom-call | tf_op jit(solution)/shard_map/pack_edges/pallas_call | solution.py:530
  1.5 3.0 %collective-permute-start = (f32[24,128]{1,0:T(8,128)S(1)}, f32[24,128]{1,0:T(8,128)S(1)}, u32[]{:S(2)}, u32[]{:S(2)}) collective-permute-start(f32[24,128]{1,0:T(8,128)S(1)} %get-tuple-element.32), channel_id=1, source_target_pairs={{0,1},{1,2},{2,3},{3,4},{4,5},{5,6},{6,7},{7,0},{8,9},{9,10},{10,1... | collective-permute-start | bytes 36872 | tf_op jit(solution)/shard_map/ppermute | solution.py:550
  4.5 3.1 %collective-permute-start.1 = (f32[24,128]{1,0:T(8,128)S(1)}, f32[24,128]{1,0:T(8,128)S(1)}, u32[]{:S(2)}, u32[]{:S(2)}) collective-permute-start(f32[24,128]{1,0:T(8,128)S(1)} %get-tuple-element.33), channel_id=1, source_target_pairs={{1,0},{2,1},{3,2},{4,3},{5,4},{6,5},{7,6},{0,7},{9,8},{10,9},{11,1... | collective-permute-start | bytes 36872 | tf_op jit(solution)/shard_map/ppermute | solution.py:551
  7.6 4.1 %smooth_inside.1 = (f32[192,8,128]{2,1,0:T(8,128)S(1)}, f32[8,8,256]{2,1,0:T(8,128)S(1)}, f32[32,128]{1,0:T(8,128)S(1)}, s32[16,128]{1,0:T(8,128)S(1)}, bf16[256,128,128]{2,1,0:T(8,128)(2,1)S(1)}) custom-call(f32[1664,128]{1,0:T(8,128)S(1)} %bitcast.4, f32[96,256]{1,0:T(8,128)S(1)} %get-tuple-element.29.rates, f32[96,256]{1,0:T(8,128)S(1)} %get-tuple-element.30.area, ...), custom_call_target="tpu_custom_call" | custom-call | bytes 12582912 | tf_op jit(solution)/shard_map/smooth_inside/pallas_call | solution.py:554
  11.6 0.0 collective-permute-done.west
  11.7 0.0 collective-permute-done.1.east
  11.7 0.1 join_corners.1
  11.7 0.7 %collective-permute-start.2 = (f32[24,256]{1,0:T(8,128)S(1)}, f32[24,256]{1,0:T(8,128)S(1)}, u32[]{:S(2)}, u32[]{:S(2)}) collective-permute-start(f32[24,256]{1,0:T(8,128)S(1)} %get-tuple-element.37), channel_id=1, source_target_pairs={{0,24},{8,16},{16,8},{24,0},{1,25},{9,17},{17,9},{25,1},{2,26},{10... | collective-permute-start | bytes 73736 | tf_op jit(solution)/shard_map/ppermute | solution.py:593
  12.4 1.1 %collective-permute-start.3 = (f32[24,256]{1,0:T(8,128)S(1)}, f32[24,256]{1,0:T(8,128)S(1)}, u32[]{:S(2)}, u32[]{:S(2)}) collective-permute-start(f32[24,256]{1,0:T(8,128)S(1)} %get-tuple-element.38), channel_id=1, source_target_pairs={{0,8},{8,0},{16,24},{24,16},{1,9},{9,1},{17,25},{25,17},{2,10},{10... | collective-permute-start | bytes 73736 | tf_op jit(solution)/shard_map/ppermute | solution.py:594
  13.5 1.8 %multiply_inside.1 = (f32[256,8,128]{2,1,0:T(8,128)S(1)}, f32[192,8,128]{2,1,0:T(8,128)S(1)}) custom-call(f32[24,128]{1,0:T(8,128)S(1)} %collective-permute-done.1.east, f32[24,128]{1,0:T(8,128)S(1)} %collective-permute-done.west, s32[16,128]{1,0:T(8,128)S(1)} %get-tuple-element.47.table_vmem, ...), custom_call_target="tpu_custom_call", output_to_operand_aliasing={{1}: (6, {})} | custom-call | flops 33554432 | bytes 4194304 | tf_op jit(solution)/shard_map/multiply_inside/pallas_call | solution.py:614
  15.3 0.0 collective-permute-done.2.rows_odd
  15.3 0.0 collective-permute-done.3.rows_even
  15.3 1.3 %add_edges.1 = (f32[256,8,128]{2,1,0:T(8,128)S(1)}, f32[192,8,128]{2,1,0:T(8,128)S(1)}) custom-call(f32[24,256]{1,0:T(8,128)S(1)} %collective-permute-done.2.rows_odd, f32[24,256]{1,0:T(8,128)S(1)} %collective-permute-done.3.rows_even, s32[16,128]{1,0:T(8,128)S(1)} %get-tuple-element.47.table_vmem, ...), custom_call_target="tpu_custom_call", output_to_operand_aliasing={{0}: (9, {}), {1}: (10, {})} | custom-call | tf_op jit(solution)/shard_map/add_edges/pallas_call | solution.py:627
  16.6 0.1 fusion.2
  16.7 0.1 collective-permute-start.4
  16.8 0.5 %collective-permute-start.5 = (f32[128,8,128]{2,1,0:T(8,128)S(1)}, f32[128,8,128]{2,1,0:T(8,128)S(1)}, u32[]{:S(2)}, u32[]{:S(2)}) collective-permute-start(f32[128,8,128]{2,1,0:T(8,128)S(1)} %get-tuple-element.55), channel_id=1, source_target_pairs={{0,8},{8,0},{16,24},{24,16},{1,9},{9,1},{17,25},{25,17},{2,10},{10... | collective-permute-start | bytes 1572872 | tf_op jit(solution)/shard_map/ppermute | solution.py:640
  17.3 1.2 %multiply_sent.1 = f32[128,8,128]{2,1,0:T(8,128)S(1)} custom-call(s32[16,128]{1,0:T(8,128)S(1)} %get-tuple-element.47.table_vmem, f32[192,8,128]{2,1,0:T(8,128)S(1)} %get-tuple-element.45.blocks, bf16[256,128,128]{2,1,0:T(8,128)(2,1)S(1)} %get-tuple-element.40.held), custom_call_target="tpu_custom_call" | custom-call | flops 33554432 | bytes 4194304 | tf_op jit(solution)/shard_map/multiply_sent/pallas_call | solution.py:600
  18.5 0.0 copy-start
  18.5 0.1 collective-permute-done.4
  18.7 0.1 add.48
  18.8 0.1 collective-permute-start.6
  18.8 1.5 %multiply_kept.1 = f32[128,8,128]{2,1,0:T(8,128)S(1)} custom-call(s32[16,128]{1,0:T(8,128)S(1)} %get-tuple-element.47.table_vmem, f32[192,8,128]{2,1,0:T(8,128)S(1)} %get-tuple-element.45.blocks, bf16[256,128,128]{2,1,0:T(8,128)(2,1)S(1)} %get-tuple-element.40.held), custom_call_target="tpu_custom_call" | custom-call | flops 33554432 | bytes 4194304 | tf_op jit(solution)/shard_map/multiply_kept/pallas_call | solution.py:600
  20.3 0.0 collective-permute-done.5
  20.4 7.6 %collective-permute-done.6 = f32[128,8,128]{2,1,0:T(8,128)S(1)} collective-permute-done((f32[128,8,128]{2,1,0:T(8,128)S(1)}, f32[128,8,128]{2,1,0:T(8,128)S(1)}, u32[]{:S(2)}, u32[]{:S(2)}) %collective-permute-start.6) | collective-permute-done | bytes 524320 | tf_op jit(solution)/shard_map/ppermute | solution.py:489
  28.0 0.1 slice_add_fusion.6
  28.1 0.6 %collective-permute-start.7 = (f32[32,8,128]{2,1,0:T(8,128)S(1)}, f32[32,8,128]{2,1,0:T(8,128)S(1)}, u32[]{:S(2)}, u32[]{:S(2)}) collective-permute-start(f32[32,8,128]{2,1,0:T(8,128)S(1)} %get-tuple-element.48), channel_id=1, source_target_pairs={{0,18},{1,19},{2,16},{3,17},{4,22},{5,23},{6,20},{7,21},{8,11},{9,... | collective-permute-start | bytes 393224 | tf_op jit(solution)/shard_map/ppermute | solution.py:489
  28.7 0.9 %collective-permute-start.8 = (f32[32,8,128]{2,1,0:T(8,128)S(1)}, f32[32,8,128]{2,1,0:T(8,128)S(1)}, u32[]{:S(2)}, u32[]{:S(2)}) collective-permute-start(f32[32,8,128]{2,1,0:T(8,128)S(1)} %get-tuple-element.49), channel_id=1, source_target_pairs={{0,16},{1,17},{2,18},{3,19},{4,20},{5,21},{6,22},{7,23},{8,10},{9,... | collective-permute-start | bytes 393224 | tf_op jit(solution)/shard_map/ppermute | solution.py:489
  29.6 2.1 %collective-permute-start.9 = (f32[32,8,128]{2,1,0:T(8,128)S(1)}, f32[32,8,128]{2,1,0:T(8,128)S(1)}, u32[]{:S(2)}, u32[]{:S(2)}) collective-permute-start(f32[32,8,128]{2,1,0:T(8,128)S(1)} %get-tuple-element.50), channel_id=1, source_target_pairs={{0,2},{1,3},{2,0},{3,1},{4,6},{5,7},{6,4},{7,5},{8,9},{9,8},{10,11... | collective-permute-start | bytes 393224 | tf_op jit(solution)/shard_map/ppermute | solution.py:489
  31.7 2.5 %collective-permute-done.7 = f32[32,8,128]{2,1,0:T(8,128)S(1)} collective-permute-done((f32[32,8,128]{2,1,0:T(8,128)S(1)}, f32[32,8,128]{2,1,0:T(8,128)S(1)}, u32[]{:S(2)}, u32[]{:S(2)}) %collective-permute-start.7) | collective-permute-done | bytes 131104 | tf_op jit(solution)/shard_map/ppermute | solution.py:489
  34.1 1.0 %collective-permute-done.8 = f32[32,8,128]{2,1,0:T(8,128)S(1)} collective-permute-done((f32[32,8,128]{2,1,0:T(8,128)S(1)}, f32[32,8,128]{2,1,0:T(8,128)S(1)}, u32[]{:S(2)}, u32[]{:S(2)}) %collective-permute-start.8) | collective-permute-done | bytes 131104 | tf_op jit(solution)/shard_map/ppermute | solution.py:489
  35.1 0.3 collective-permute-done.9
  35.4 1.7 %collective-permute-start.10 = (f32[16,8,128]{2,1,0:T(8,128)S(1)}, f32[16,8,128]{2,1,0:T(8,128)S(1)}, u32[]{:S(2)}, u32[]{:S(2)}) collective-permute-start(f32[16,8,128]{2,1,0:T(8,128)S(1)} %slice_add_fusion.8), channel_id=1, source_target_pairs={{0,4},{1,5},{2,6},{3,7},{4,0},{5,1},{6,2},{7,3},{8,12},{9,13},{10,... | collective-permute-start | bytes 196616 | tf_op jit(solution)/shard_map/ppermute | solution.py:489
  37.1 3.6 %collective-permute-done.10 = f32[16,8,128]{2,1,0:T(8,128)S(1)} collective-permute-done((f32[16,8,128]{2,1,0:T(8,128)S(1)}, f32[16,8,128]{2,1,0:T(8,128)S(1)}, u32[]{:S(2)}, u32[]{:S(2)}) %collective-permute-start.10) | collective-permute-done | bytes 65568 | tf_op jit(solution)/shard_map/ppermute | solution.py:489
  40.6 0.0 copy-done
  40.6 0.7 %fusion.1 = f32[16,8,128]{2,1,0:T(8,128)} fusion(f32[16,8,128]{2,1,0:T(8,128)S(1)} %collective-permute-done.10, f32[32,8,128]{2,1,0:T(8,128)S(1)} %collective-permute-done.9, f32[32,8,128]{2,1,0:T(8,128)S(1)} %collective-permute-done.8, f32[32,8,128]{2,1,0:T(8,128)S(1)} %collective-permute-done.7, f32[32,8,128]{2,1,0:T(8,128)S(1)} %get-tuple-element.51, ...), kind=kLoop, calls=%fused_computation.13 | loop fusion | flops 81920 | bytes 401408 | tf_op jit(solution)/shard_map/div | solution.py:645
  (1 shorter events, 0.0 us)
Async XLA Ops:
  1.5 10.2 %collective-permute-start = (f32[24,128]{1,0:T(8,128)S(1)}, f32[24,128]{1,0:T(8,128)S(1)}, u32[]{:S(2)}, u32[]{:S(2)}) collective-permute-start(f32[24,128]{1,0:T(8,128)S(1)} %get-tuple-element.32), channel_id=1, source_target_pairs={{0,1},{1,2},{2,3},{3,4},{4,5},{5,6},{6,7},{7,0},{8,9},{9,10},{10,1... | collective-permute-start | bytes 36872 | tf_op jit(solution)/shard_map/ppermute | solution.py:550
  4.5 7.2 %collective-permute-start.1 = (f32[24,128]{1,0:T(8,128)S(1)}, f32[24,128]{1,0:T(8,128)S(1)}, u32[]{:S(2)}, u32[]{:S(2)}) collective-permute-start(f32[24,128]{1,0:T(8,128)S(1)} %get-tuple-element.33), channel_id=1, source_target_pairs={{1,0},{2,1},{3,2},{4,3},{5,4},{6,5},{7,6},{0,7},{9,8},{10,9},{11,1... | collective-permute-start | bytes 36872 | tf_op jit(solution)/shard_map/ppermute | solution.py:551
  11.7 3.6 %collective-permute-start.2 = (f32[24,256]{1,0:T(8,128)S(1)}, f32[24,256]{1,0:T(8,128)S(1)}, u32[]{:S(2)}, u32[]{:S(2)}) collective-permute-start(f32[24,256]{1,0:T(8,128)S(1)} %get-tuple-element.37), channel_id=1, source_target_pairs={{0,24},{8,16},{16,8},{24,0},{1,25},{9,17},{17,9},{25,1},{2,26},{10... | collective-permute-start | bytes 73736 | tf_op jit(solution)/shard_map/ppermute | solution.py:593
  12.4 2.9 %collective-permute-start.3 = (f32[24,256]{1,0:T(8,128)S(1)}, f32[24,256]{1,0:T(8,128)S(1)}, u32[]{:S(2)}, u32[]{:S(2)}) collective-permute-start(f32[24,256]{1,0:T(8,128)S(1)} %get-tuple-element.38), channel_id=1, source_target_pairs={{0,8},{8,0},{16,24},{24,16},{1,9},{9,1},{17,25},{25,17},{2,10},{10... | collective-permute-start | bytes 73736 | tf_op jit(solution)/shard_map/ppermute | solution.py:594
  16.7 2.0 %collective-permute-start.4 = (f32[128,8,128]{2,1,0:T(8,128)S(1)}, f32[128,8,128]{2,1,0:T(8,128)S(1)}, u32[]{:S(2)}, u32[]{:S(2)}) collective-permute-start(f32[128,8,128]{2,1,0:T(8,128)S(1)} %get-tuple-element.56), channel_id=1, source_target_pairs={{0,8},{8,0},{16,24},{24,16},{1,9},{9,1},{17,25},{25,17},{2,10},{10... | collective-permute-start | bytes 1572872 | tf_op jit(solution)/shard_map/ppermute | solution.py:639
  16.8 3.6 %collective-permute-start.5 = (f32[128,8,128]{2,1,0:T(8,128)S(1)}, f32[128,8,128]{2,1,0:T(8,128)S(1)}, u32[]{:S(2)}, u32[]{:S(2)}) collective-permute-start(f32[128,8,128]{2,1,0:T(8,128)S(1)} %get-tuple-element.55), channel_id=1, source_target_pairs={{0,8},{8,0},{16,24},{24,16},{1,9},{9,1},{17,25},{25,17},{2,10},{10... | collective-permute-start | bytes 1572872 | tf_op jit(solution)/shard_map/ppermute | solution.py:640
  18.5 22.1 %copy-start = (f32[16,128]{1,0:T(8,128)S(1)}, f32[16,128]{1,0:T(8,128)}, u32[]{:S(2)}) copy-start(f32[16,128]{1,0:T(8,128)} %param.15) | copy-start | bytes 24580
  18.8 9.2 %collective-permute-start.6 = (f32[128,8,128]{2,1,0:T(8,128)S(1)}, f32[128,8,128]{2,1,0:T(8,128)S(1)}, u32[]{:S(2)}, u32[]{:S(2)}) collective-permute-start(f32[128,8,128]{2,1,0:T(8,128)S(1)} %add.48), channel_id=1, source_target_pairs={{0,1},{1,0},{2,3},{3,2},{4,5},{5,4},{6,7},{7,6},{8,24},{9,25},{10,... | collective-permute-start | bytes 1572872 | tf_op jit(solution)/shard_map/ppermute | solution.py:489
  28.1 6.0 %collective-permute-start.7 = (f32[32,8,128]{2,1,0:T(8,128)S(1)}, f32[32,8,128]{2,1,0:T(8,128)S(1)}, u32[]{:S(2)}, u32[]{:S(2)}) collective-permute-start(f32[32,8,128]{2,1,0:T(8,128)S(1)} %get-tuple-element.48), channel_id=1, source_target_pairs={{0,18},{1,19},{2,16},{3,17},{4,22},{5,23},{6,20},{7,21},{8,11},{9,... | collective-permute-start | bytes 393224 | tf_op jit(solution)/shard_map/ppermute | solution.py:489
  28.7 6.4 %collective-permute-start.8 = (f32[32,8,128]{2,1,0:T(8,128)S(1)}, f32[32,8,128]{2,1,0:T(8,128)S(1)}, u32[]{:S(2)}, u32[]{:S(2)}) collective-permute-start(f32[32,8,128]{2,1,0:T(8,128)S(1)} %get-tuple-element.49), channel_id=1, source_target_pairs={{0,16},{1,17},{2,18},{3,19},{4,20},{5,21},{6,22},{7,23},{8,10},{9,... | collective-permute-start | bytes 393224 | tf_op jit(solution)/shard_map/ppermute | solution.py:489
  29.6 5.8 %collective-permute-start.9 = (f32[32,8,128]{2,1,0:T(8,128)S(1)}, f32[32,8,128]{2,1,0:T(8,128)S(1)}, u32[]{:S(2)}, u32[]{:S(2)}) collective-permute-start(f32[32,8,128]{2,1,0:T(8,128)S(1)} %get-tuple-element.50), channel_id=1, source_target_pairs={{0,2},{1,3},{2,0},{3,1},{4,6},{5,7},{6,4},{7,5},{8,9},{9,8},{10,11... | collective-permute-start | bytes 393224 | tf_op jit(solution)/shard_map/ppermute | solution.py:489
  35.4 5.2 %collective-permute-start.10 = (f32[16,8,128]{2,1,0:T(8,128)S(1)}, f32[16,8,128]{2,1,0:T(8,128)S(1)}, u32[]{:S(2)}, u32[]{:S(2)}) collective-permute-start(f32[16,8,128]{2,1,0:T(8,128)S(1)} %slice_add_fusion.8), channel_id=1, source_target_pairs={{0,4},{1,5},{2,6},{3,7},{4,0},{5,1},{6,2},{7,3},{8,12},{9,13},{10,... | collective-permute-start | bytes 196616 | tf_op jit(solution)/shard_map/ppermute | solution.py:489
where the time goes:
time: 41.4 us; the launch traced here: 41.3 us
  waiting for transfers between devices  15.1 us (36%)
  starting transfers between devices  13.7 us (33%)
  Pallas kernels  11.4 us (28%)
  other arithmetic  0.86 us (2%)
    ppermute x5, waiting for transfers between devices, swap_parts(): lax.ppermute(part, ('ty', 'tx'), [(i, partner(i, q)) for i in range(n_ty...  14.9 us
    ppermute x5, starting transfers between devices, swap_parts(): lax.ppermute(part, ('ty', 'tx'), [(i, partner(i, q)) for i in range(n_ty...  5.3 us
    pallas_call x1, Pallas kernels, on_device(): pl.pallas_call(functools.partial(smooth_kernel, rows, sizes), out_shape=(...  4.05 us
    ppermute x1, starting transfers between devices, on_device(): lax.ppermute(west_cols, 'tx', [((i + 1) % n_tx, i) for i in range(n_tx)])  3.1 us
    ppermute x1, starting transfers between devices, on_device(): lax.ppermute(east_cols, 'tx', [(i, (i + 1) % n_tx) for i in range(n_tx)])  2.99 us
    pallas_call x2, Pallas kernels, sums_of(): pl.pallas_call(functools.partial(sum_kernel, kind, first_row), out_shape=...  2.74 us
    pallas_call x1, Pallas kernels, on_device(): pl.pallas_call(functools.partial(inner_kernel, rows, width // BW), out_sh...  1.77 us
    pallas_call x1, Pallas kernels, on_device(): pl.pallas_call(functools.partial(pack_kernel, rows), out_shape=(edge_cols...  1.48 us
  transfers between devices with their start and end apart: 11, of which 6 were waited for; matrix products, arithmetic and copies ran while one was open for 0% of the time, Pallas kernels for 21%

commit v1 on v0

--- a/solution.py
+++ b/solution.py
@@ -36,10 +36,12 @@
     west_cols, east_cols, first_rows, last_rows, own_cols, narrow, rates, area, sems,
 ):
     width = rates.shape[1]
-    parts, count = narrow.shape[:2]
+    parts, count = width // LANES, fields_hbm.shape[0]
     copies = [
         pltpu.make_async_copy(
-            fields_hbm.at[:, :, pl.ds(h * LANES, LANES)], narrow.at[h, :, pl.ds(0, rows)], sems.at[2 + h]
+            fields_hbm.at[:, :, pl.ds(h * LANES, LANES)],
+            narrow.at[pl.ds(h * count, count), pl.ds(0, rows)],
+            sems.at[2 + h],
         )
         for h in range(parts)
     ]
@@ -50,7 +52,7 @@
         for r in range(HALO):
             for h in range(parts):
                 for v in range(count):
-                    line = narrow[h, v, start + r : start + r + 1, :]
+                    line = narrow[h * count + v, start + r : start + r + 1, :]
                     out[r * 16 + v : r * 16 + v + 1, h * LANES : (h + 1) * LANES] = line
             out[r * 16 + SUB : r * 16 + 16, :] = jnp.broadcast_to(rates[start + r : start + r + 1, :], (SUB, width))
     pad = jnp.zeros((LANES - rows, LANES), jnp.float32)
@@ -59,7 +61,7 @@
         if v == count:
             west, east, high = rates[:, :LANES], rates[:, width - LANES :], SUB
         else:
-            west, east, high = narrow[0, v, :rows, :], narrow[parts - 1, v, :rows, :], 1
+            west, east, high = narrow[v, :rows, :], narrow[(parts - 1) * count + v, :rows, :], 1
         sides = jnp.concatenate([jnp.where(left, west, east), pad], axis=0).T
         for c in range(EDGE):
             for side, line in ((0, sides[c : c + 1, :]), (1, sides[LANES - EDGE + c : LANES - EDGE + c + 1, :])):
@@ -202,7 +204,7 @@
     width = rates.shape[1]
     count = blocks.shape[1]
     parts = width // LANES
-    pitch = narrow.shape[0] // (parts * count)
+    pitch = narrow.shape[0] // (parts * count + 1)
     lines = owner.shape[0]
     copies = [
         pltpu.make_async_copy(pairs_hbm, pairs, sems.at[0]),
@@ -535,7 +537,7 @@
             edge_rows,
             edge_rows,
             pltpu.VMEM((2 * EDGE * 16, LANES), jnp.float32),
-            pltpu.VMEM((parts, count, pitch, LANES), jnp.float32),
+            pltpu.VMEM((parts * count + 1, pitch, LANES), jnp.float32),
             tile,
             tile,
         ),
@@ -545,7 +547,7 @@
         compiler_params=pltpu.CompilerParams(vmem_limit_bytes=16 << 20),
         name="pack_edges",
     )(source_fields, diffusivity, cell_area)
-    narrow = narrow.reshape(parts * count * pitch, LANES)
+    narrow = narrow.reshape((parts * count + 1) * pitch, LANES)
 
     west = lax.ppermute(east_cols, "tx", [(i, (i + 1) % n_tx) for i in range(n_tx)])
     east = lax.ppermute(west_cols, "tx", [((i + 1) % n_tx, i) for i in range(n_tx)])

time: 41.4 us -> 42.3 us (1.022)
  waiting for transfers between devices: 15.1 us -> 16.2 us
    ppermute x5, waiting for transfers between devices: 14.9 us -> 16.1 us  [swap_parts(): lax.ppermute(part, ('ty', 'tx'), [(i, partner(i, q)) for i in range(n_ty...]
  transfers between devices with their start and end apart: 11 -> 11, of which waited for: 6 -> 5; matrix products, arithmetic and copies ran while one was open for 0% -> 0% of each run, Pallas kernels for 21% -> 20%
where the time goes in v1:
time: 42.3 us; the launch traced here: 42.1 us
  waiting for transfers between devices  16.2 us (38%)
  starting transfers between devices  13.8 us (33%)
  Pallas kernels  11.1 us (26%)
  other arithmetic  0.87 us (2%)
    ppermute x5, waiting for transfers between devices, swap_parts(): lax.ppermute(part, ('ty', 'tx'), [(i, partner(i, q)) for i in range(n_ty...  16.1 us
    ppermute x5, starting transfers between devices, swap_parts(): lax.ppermute(part, ('ty', 'tx'), [(i, partner(i, q)) for i in range(n_ty...  5.3 us
    pallas_call x1, Pallas kernels, on_device(): pl.pallas_call(functools.partial(smooth_kernel, rows, sizes), out_shape=(...  4.05 us
    ppermute x1, starting transfers between devices, on_device(): lax.ppermute(west_cols, 'tx', [((i + 1) % n_tx, i) for i in range(n_tx)])  3.1 us
    ppermute x1, starting transfers between devices, on_device(): lax.ppermute(east_cols, 'tx', [(i, (i + 1) % n_tx) for i in range(n_tx)])  2.99 us
    pallas_call x2, Pallas kernels, sums_of(): pl.pallas_call(functools.partial(sum_kernel, kind, first_row), out_shape=...  2.74 us
    pallas_call x1, Pallas kernels, on_device(): pl.pallas_call(functools.partial(inner_kernel, rows, width // BW), out_sh...  1.5 us
    pallas_call x1, Pallas kernels, on_device(): pl.pallas_call(functools.partial(pack_kernel, rows), out_shape=(edge_cols...  1.48 us
  transfers between devices with their start and end apart: 11, of which 5 were waited for; matrix products, arithmetic and copies ran while one was open for 0% of the time, Pallas kernels for 20%

profile of v1, /device:TPU:0, one launch (start us, length us, event | category | flops | bytes accessed | tf_op | source)
XLA Modules:
  0.0 42.1 jit_solution(9867724428072652768)
XLA Ops:
  0.0 1.5 %pack_edges.1 = (f32[24,128]{1,0:T(8,128)S(1)}, f32[24,128]{1,0:T(8,128)S(1)}, f32[32,256]{1,0:T(8,128)S(1)}, f32[32,256]{1,0:T(8,128)S(1)}, f32[128,128]{1,0:T(...) custom-call(f32[8,96,256]{2,1,0:T(8,128)} %fields_hbm.1, ...), custom_call_target="tpu_custom_call" | custom-call | tf_op jit(solution)/shard_map/pack_edges/pallas_call | solution.py:532
  1.5 3.0 %collective-permute-start = (f32[24,128]{1,0:T(8,128)S(1)}, f32[24,128]{1,0:T(8,128)S(1)}, u32[]{:S(2)}, u32[]{:S(2)}) collective-permute-start(f32[24,128]{1,0:T(8,128)S(1)} %get-tuple-element.32), channel_id=1, source_target_pairs={{0,1},{1,2},{2,3},{3,4},{4,5},{5,6},{6,7},{7,0},{8,9},{9,10},{10,1... | collective-permute-start | bytes 36872 | tf_op jit(solution)/shard_map/ppermute | solution.py:552
  4.5 3.1 %collective-permute-start.1 = (f32[24,128]{1,0:T(8,128)S(1)}, f32[24,128]{1,0:T(8,128)S(1)}, u32[]{:S(2)}, u32[]{:S(2)}) collective-permute-start(f32[24,128]{1,0:T(8,128)S(1)} %get-tuple-element.33), channel_id=1, source_target_pairs={{1,0},{2,1},{3,2},{4,3},{5,4},{6,5},{7,6},{0,7},{9,8},{10,9},{11,1... | collective-permute-start | bytes 36872 | tf_op jit(solution)/shard_map/ppermute | solution.py:553
  7.6 4.1 %smooth_inside.1 = (f32[192,8,128]{2,1,0:T(8,128)S(1)}, f32[8,8,256]{2,1,0:T(8,128)S(1)}, f32[32,128]{1,0:T(8,128)S(1)}, s32[16,128]{1,0:T(8,128)S(1)}, bf16[256,128,128]{2,1,0:T(8,128)(2,1)S(1)}) custom-call(f32[1768,128]{1,0:T(8,128)S(1)} %bitcast.4, f32[96,256]{1,0:T(8,128)S(1)} %get-tuple-element.29.rates, f32[96,256]{1,0:T(8,128)S(1)} %get-tuple-element.30.area, ...), custom_call_target="tpu_custom_call" | custom-call | bytes 12582912 | tf_op jit(solution)/shard_map/smooth_inside/pallas_call | solution.py:556
  11.6 0.0 collective-permute-done.west
  11.7 0.0 collective-permute-done.1.east
  11.7 0.1 join_corners.1
  11.7 0.7 %collective-permute-start.2 = (f32[24,256]{1,0:T(8,128)S(1)}, f32[24,256]{1,0:T(8,128)S(1)}, u32[]{:S(2)}, u32[]{:S(2)}) collective-permute-start(f32[24,256]{1,0:T(8,128)S(1)} %get-tuple-element.37), channel_id=1, source_target_pairs={{0,24},{8,16},{16,8},{24,0},{1,25},{9,17},{17,9},{25,1},{2,26},{10... | collective-permute-start | bytes 73736 | tf_op jit(solution)/shard_map/ppermute | solution.py:595
  12.4 1.1 %collective-permute-start.3 = (f32[24,256]{1,0:T(8,128)S(1)}, f32[24,256]{1,0:T(8,128)S(1)}, u32[]{:S(2)}, u32[]{:S(2)}) collective-permute-start(f32[24,256]{1,0:T(8,128)S(1)} %get-tuple-element.38), channel_id=1, source_target_pairs={{0,8},{8,0},{16,24},{24,16},{1,9},{9,1},{17,25},{25,17},{2,10},{10... | collective-permute-start | bytes 73736 | tf_op jit(solution)/shard_map/ppermute | solution.py:596
  13.5 1.5 %multiply_inside.1 = (f32[256,8,128]{2,1,0:T(8,128)S(1)}, f32[192,8,128]{2,1,0:T(8,128)S(1)}) custom-call(f32[24,128]{1,0:T(8,128)S(1)} %collective-permute-done.1.east, f32[24,128]{1,0:T(8,128)S(1)} %collective-permute-done.west, s32[16,128]{1,0:T(8,128)S(1)} %get-tuple-element.47.table_vmem, ...), custom_call_target="tpu_custom_call", output_to_operand_aliasing={{1}: (6, {})} | custom-call | flops 33554432 | bytes 4194304 | tf_op jit(solution)/shard_map/multiply_inside/pallas_call | solution.py:616
  15.0 0.0 collective-permute-done.2.rows_odd
  15.1 0.0 collective-permute-done.3.rows_even
  15.1 1.3 %add_edges.1 = (f32[256,8,128]{2,1,0:T(8,128)S(1)}, f32[192,8,128]{2,1,0:T(8,128)S(1)}) custom-call(f32[24,256]{1,0:T(8,128)S(1)} %collective-permute-done.2.rows_odd, f32[24,256]{1,0:T(8,128)S(1)} %collective-permute-done.3.rows_even, s32[16,128]{1,0:T(8,128)S(1)} %get-tuple-element.47.table_vmem, ...), custom_call_target="tpu_custom_call", output_to_operand_aliasing={{0}: (9, {}), {1}: (10, {})} | custom-call | tf_op jit(solution)/shard_map/add_edges/pallas_call | solution.py:629
  16.4 0.1 fusion.2
  16.5 0.3 collective-permute-start.4
  16.8 0.3 collective-permute-start.5
  17.0 1.5 %multiply_sent.1 = f32[128,8,128]{2,1,0:T(8,128)S(1)} custom-call(s32[16,128]{1,0:T(8,128)S(1)} %get-tuple-element.47.table_vmem, f32[192,8,128]{2,1,0:T(8,128)S(1)} %get-tuple-element.45.blocks, bf16[256,128,128]{2,1,0:T(8,128)(2,1)S(1)} %get-tuple-element.40.held), custom_call_target="tpu_custom_call" | custom-call | flops 33554432 | bytes 4194304 | tf_op jit(solution)/shard_map/multiply_sent/pallas_call | solution.py:602
  18.6 0.0 copy-start
  18.6 0.0 collective-permute-done.4
  18.6 0.1 add.48
  18.7 0.1 collective-permute-start.6
  18.7 1.2 %multiply_kept.1 = f32[128,8,128]{2,1,0:T(8,128)S(1)} custom-call(s32[16,128]{1,0:T(8,128)S(1)} %get-tuple-element.47.table_vmem, f32[192,8,128]{2,1,0:T(8,128)S(1)} %get-tuple-element.45.blocks, bf16[256,128,128]{2,1,0:T(8,128)(2,1)S(1)} %get-tuple-element.40.held), custom_call_target="tpu_custom_call" | custom-call | flops 33554432 | bytes 4194304 | tf_op jit(solution)/shard_map/multiply_kept/pallas_call | solution.py:602
  20.0 0.0 collective-permute-done.5
  20.0 7.9 %collective-permute-done.6 = f32[128,8,128]{2,1,0:T(8,128)S(1)} collective-permute-done((f32[128,8,128]{2,1,0:T(8,128)S(1)}, f32[128,8,128]{2,1,0:T(8,128)S(1)}, u32[]{:S(2)}, u32[]{:S(2)}) %collective-permute-start.6) | collective-permute-done | bytes 524320 | tf_op jit(solution)/shard_map/ppermute | solution.py:491
  27.9 0.1 slice_add_fusion.6
  28.0 0.9 %collective-permute-start.7 = (f32[32,8,128]{2,1,0:T(8,128)S(1)}, f32[32,8,128]{2,1,0:T(8,128)S(1)}, u32[]{:S(2)}, u32[]{:S(2)}) collective-permute-start(f32[32,8,128]{2,1,0:T(8,128)S(1)} %get-tuple-element.48), channel_id=1, source_target_pairs={{0,18},{1,19},{2,16},{3,17},{4,22},{5,23},{6,20},{7,21},{8,11},{9,... | collective-permute-start | bytes 393224 | tf_op jit(solution)/shard_map/ppermute | solution.py:491
  28.9 0.9 %collective-permute-start.8 = (f32[32,8,128]{2,1,0:T(8,128)S(1)}, f32[32,8,128]{2,1,0:T(8,128)S(1)}, u32[]{:S(2)}, u32[]{:S(2)}) collective-permute-start(f32[32,8,128]{2,1,0:T(8,128)S(1)} %get-tuple-element.49), channel_id=1, source_target_pairs={{0,16},{1,17},{2,18},{3,19},{4,20},{5,21},{6,22},{7,23},{8,10},{9,... | collective-permute-start | bytes 393224 | tf_op jit(solution)/shard_map/ppermute | solution.py:491
  29.7 1.8 %collective-permute-start.9 = (f32[32,8,128]{2,1,0:T(8,128)S(1)}, f32[32,8,128]{2,1,0:T(8,128)S(1)}, u32[]{:S(2)}, u32[]{:S(2)}) collective-permute-start(f32[32,8,128]{2,1,0:T(8,128)S(1)} %get-tuple-element.50), channel_id=1, source_target_pairs={{0,2},{1,3},{2,0},{3,1},{4,6},{5,7},{6,4},{7,5},{8,9},{9,8},{10,11... | collective-permute-start | bytes 393224 | tf_op jit(solution)/shard_map/ppermute | solution.py:491
  31.6 2.5 %collective-permute-done.7 = f32[32,8,128]{2,1,0:T(8,128)S(1)} collective-permute-done((f32[32,8,128]{2,1,0:T(8,128)S(1)}, f32[32,8,128]{2,1,0:T(8,128)S(1)}, u32[]{:S(2)}, u32[]{:S(2)}) %collective-permute-start.7) | collective-permute-done | bytes 131104 | tf_op jit(solution)/shard_map/ppermute | solution.py:491
  34.1 1.2 %collective-permute-done.8 = f32[32,8,128]{2,1,0:T(8,128)S(1)} collective-permute-done((f32[32,8,128]{2,1,0:T(8,128)S(1)}, f32[32,8,128]{2,1,0:T(8,128)S(1)}, u32[]{:S(2)}, u32[]{:S(2)}) %collective-permute-start.8) | collective-permute-done | bytes 131104 | tf_op jit(solution)/shard_map/ppermute | solution.py:491
  35.3 0.3 collective-permute-done.9
  35.5 1.7 %collective-permute-start.10 = (f32[16,8,128]{2,1,0:T(8,128)S(1)}, f32[16,8,128]{2,1,0:T(8,128)S(1)}, u32[]{:S(2)}, u32[]{:S(2)}) collective-permute-start(f32[16,8,128]{2,1,0:T(8,128)S(1)} %slice_add_fusion.8), channel_id=1, source_target_pairs={{0,4},{1,5},{2,6},{3,7},{4,0},{5,1},{6,2},{7,3},{8,12},{9,13},{10,... | collective-permute-start | bytes 196616 | tf_op jit(solution)/shard_map/ppermute | solution.py:491
  37.2 4.3 %collective-permute-done.10 = f32[16,8,128]{2,1,0:T(8,128)S(1)} collective-permute-done((f32[16,8,128]{2,1,0:T(8,128)S(1)}, f32[16,8,128]{2,1,0:T(8,128)S(1)}, u32[]{:S(2)}, u32[]{:S(2)}) %collective-permute-start.10) | collective-permute-done | bytes 65568 | tf_op jit(solution)/shard_map/ppermute | solution.py:491
  41.5 0.0 copy-done
  41.5 0.7 %fusion.1 = f32[16,8,128]{2,1,0:T(8,128)} fusion(f32[16,8,128]{2,1,0:T(8,128)S(1)} %collective-permute-done.10, f32[32,8,128]{2,1,0:T(8,128)S(1)} %collective-permute-done.9, f32[32,8,128]{2,1,0:T(8,128)S(1)} %collective-permute-done.8, f32[32,8,128]{2,1,0:T(8,128)S(1)} %collective-permute-done.7, f32[32,8,128]{2,1,0:T(8,128)S(1)} %get-tuple-element.51, ...), kind=kLoop, calls=%fused_computation.13 | loop fusion | flops 81920 | bytes 401408 | tf_op jit(solution)/shard_map/div | solution.py:647
  (1 shorter events, 0.0 us)
Async XLA Ops:
  1.5 10.2 %collective-permute-start = (f32[24,128]{1,0:T(8,128)S(1)}, f32[24,128]{1,0:T(8,128)S(1)}, u32[]{:S(2)}, u32[]{:S(2)}) collective-permute-start(f32[24,128]{1,0:T(8,128)S(1)} %get-tuple-element.32), channel_id=1, source_target_pairs={{0,1},{1,2},{2,3},{3,4},{4,5},{5,6},{6,7},{7,0},{8,9},{9,10},{10,1... | collective-permute-start | bytes 36872 | tf_op jit(solution)/shard_map/ppermute | solution.py:552
  4.5 7.2 %collective-permute-start.1 = (f32[24,128]{1,0:T(8,128)S(1)}, f32[24,128]{1,0:T(8,128)S(1)}, u32[]{:S(2)}, u32[]{:S(2)}) collective-permute-start(f32[24,128]{1,0:T(8,128)S(1)} %get-tuple-element.33), channel_id=1, source_target_pairs={{1,0},{2,1},{3,2},{4,3},{5,4},{6,5},{7,6},{0,7},{9,8},{10,9},{11,1... | collective-permute-start | bytes 36872 | tf_op jit(solution)/shard_map/ppermute | solution.py:553
  11.7 3.3 %collective-permute-start.2 = (f32[24,256]{1,0:T(8,128)S(1)}, f32[24,256]{1,0:T(8,128)S(1)}, u32[]{:S(2)}, u32[]{:S(2)}) collective-permute-start(f32[24,256]{1,0:T(8,128)S(1)} %get-tuple-element.37), channel_id=1, source_target_pairs={{0,24},{8,16},{16,8},{24,0},{1,25},{9,17},{17,9},{25,1},{2,26},{10... | collective-permute-start | bytes 73736 | tf_op jit(solution)/shard_map/ppermute | solution.py:595
  12.4 2.6 %collective-permute-start.3 = (f32[24,256]{1,0:T(8,128)S(1)}, f32[24,256]{1,0:T(8,128)S(1)}, u32[]{:S(2)}, u32[]{:S(2)}) collective-permute-start(f32[24,256]{1,0:T(8,128)S(1)} %get-tuple-element.38), channel_id=1, source_target_pairs={{0,8},{8,0},{16,24},{24,16},{1,9},{9,1},{17,25},{25,17},{2,10},{10... | collective-permute-start | bytes 73736 | tf_op jit(solution)/shard_map/ppermute | solution.py:596
  16.5 2.1 %collective-permute-start.4 = (f32[128,8,128]{2,1,0:T(8,128)S(1)}, f32[128,8,128]{2,1,0:T(8,128)S(1)}, u32[]{:S(2)}, u32[]{:S(2)}) collective-permute-start(f32[128,8,128]{2,1,0:T(8,128)S(1)} %get-tuple-element.56), channel_id=1, source_target_pairs={{0,8},{8,0},{16,24},{24,16},{1,9},{9,1},{17,25},{25,17},{2,10},{10... | collective-permute-start | bytes 1572872 | tf_op jit(solution)/shard_map/ppermute | solution.py:641
  16.8 3.2 %collective-permute-start.5 = (f32[128,8,128]{2,1,0:T(8,128)S(1)}, f32[128,8,128]{2,1,0:T(8,128)S(1)}, u32[]{:S(2)}, u32[]{:S(2)}) collective-permute-start(f32[128,8,128]{2,1,0:T(8,128)S(1)} %get-tuple-element.55), channel_id=1, source_target_pairs={{0,8},{8,0},{16,24},{24,16},{1,9},{9,1},{17,25},{25,17},{2,10},{10... | collective-permute-start | bytes 1572872 | tf_op jit(solution)/shard_map/ppermute | solution.py:642
  18.6 22.9 %copy-start = (f32[16,128]{1,0:T(8,128)S(1)}, f32[16,128]{1,0:T(8,128)}, u32[]{:S(2)}) copy-start(f32[16,128]{1,0:T(8,128)} %param.15) | copy-start | bytes 24580
  18.7 9.2 %collective-permute-start.6 = (f32[128,8,128]{2,1,0:T(8,128)S(1)}, f32[128,8,128]{2,1,0:T(8,128)S(1)}, u32[]{:S(2)}, u32[]{:S(2)}) collective-permute-start(f32[128,8,128]{2,1,0:T(8,128)S(1)} %add.48), channel_id=1, source_target_pairs={{0,1},{1,0},{2,3},{3,2},{4,5},{5,4},{6,7},{7,6},{8,24},{9,25},{10,... | collective-permute-start | bytes 1572872 | tf_op jit(solution)/shard_map/ppermute | solution.py:491
  28.0 6.0 %collective-permute-start.7 = (f32[32,8,128]{2,1,0:T(8,128)S(1)}, f32[32,8,128]{2,1,0:T(8,128)S(1)}, u32[]{:S(2)}, u32[]{:S(2)}) collective-permute-start(f32[32,8,128]{2,1,0:T(8,128)S(1)} %get-tuple-element.48), channel_id=1, source_target_pairs={{0,18},{1,19},{2,16},{3,17},{4,22},{5,23},{6,20},{7,21},{8,11},{9,... | collective-permute-start | bytes 393224 | tf_op jit(solution)/shard_map/ppermute | solution.py:491
  28.9 6.4 %collective-permute-start.8 = (f32[32,8,128]{2,1,0:T(8,128)S(1)}, f32[32,8,128]{2,1,0:T(8,128)S(1)}, u32[]{:S(2)}, u32[]{:S(2)}) collective-permute-start(f32[32,8,128]{2,1,0:T(8,128)S(1)} %get-tuple-element.49), channel_id=1, source_target_pairs={{0,16},{1,17},{2,18},{3,19},{4,20},{5,21},{6,22},{7,23},{8,10},{9,... | collective-permute-start | bytes 393224 | tf_op jit(solution)/shard_map/ppermute | solution.py:491
  29.7 5.8 %collective-permute-start.9 = (f32[32,8,128]{2,1,0:T(8,128)S(1)}, f32[32,8,128]{2,1,0:T(8,128)S(1)}, u32[]{:S(2)}, u32[]{:S(2)}) collective-permute-start(f32[32,8,128]{2,1,0:T(8,128)S(1)} %get-tuple-element.50), channel_id=1, source_target_pairs={{0,2},{1,3},{2,0},{3,1},{4,6},{5,7},{6,4},{7,5},{8,9},{9,8},{10,11... | collective-permute-start | bytes 393224 | tf_op jit(solution)/shard_map/ppermute | solution.py:491
  35.5 5.9 %collective-permute-start.10 = (f32[16,8,128]{2,1,0:T(8,128)S(1)}, f32[16,8,128]{2,1,0:T(8,128)S(1)}, u32[]{:S(2)}, u32[]{:S(2)}) collective-permute-start(f32[16,8,128]{2,1,0:T(8,128)S(1)} %slice_add_fusion.8), channel_id=1, source_target_pairs={{0,4},{1,5},{2,6},{3,7},{4,0},{5,1},{6,2},{7,3},{8,12},{9,13},{10,... | collective-permute-start | bytes 196616 | tf_op jit(solution)/shard_map/ppermute | solution.py:491

commit v2 on v1

--- a/solution.py
+++ b/solution.py
@@ -137,7 +137,7 @@
     x, y, z, far = 1, 2 * n_tx, 2, 4
     others = [1 << i for i in range(3, n_tx.bit_length() - 1)] + [n_tx << i for i in range(2, n_ty.bit_length() - 1)]
     others = [[i] for i in others]
-    return [[x], [y, z], [far]] + others, [[y], [z, x], [far]] + others
+    return [[x], [z, y], [far]] + others, [[y], [z, x], [far]] + others
 
 
 def target_rows(block, owner, target, sizes):

time: 42.3 us -> 42.6 us (level)
  waiting for transfers between devices: 16.2 us -> 16.8 us
    ppermute x5, waiting for transfers between devices: 16.1 us -> 16.6 us  [swap_parts(): lax.ppermute(part, ('ty', 'tx'), [(i, partner(i, q)) for i in range(n_ty...]
  transfers between devices with their start and end apart: 11 -> 11, of which waited for: 5 -> 6; matrix products, arithmetic and copies ran while one was open for 0% -> 0% of each run, Pallas kernels for 20% -> 20%
where the time goes in v2:
time: 42.6 us; the launch traced here: 42.4 us
  waiting for transfers between devices  16.8 us (39%)
  starting transfers between devices  13.4 us (31%)
  Pallas kernels  11.1 us (26%)
  other arithmetic  0.86 us (2%)
    ppermute x5, waiting for transfers between devices, swap_parts(): lax.ppermute(part, ('ty', 'tx'), [(i, partner(i, q)) for i in range(n_ty...  16.6 us
    ppermute x5, starting transfers between devices, swap_parts(): lax.ppermute(part, ('ty', 'tx'), [(i, partner(i, q)) for i in range(n_ty...  4.98 us
    pallas_call x1, Pallas kernels, on_device(): pl.pallas_call(functools.partial(smooth_kernel, rows, sizes), out_shape=(...  4.05 us
    ppermute x1, starting transfers between devices, on_device(): lax.ppermute(west_cols, 'tx', [((i + 1) % n_tx, i) for i in range(n_tx)])  3.1 us
    ppermute x1, starting transfers between devices, on_device(): lax.ppermute(east_cols, 'tx', [(i, (i + 1) % n_tx) for i in range(n_tx)])  2.99 us
    pallas_call x2, Pallas kernels, sums_of(): pl.pallas_call(functools.partial(sum_kernel, kind, first_row), out_shape=...  2.46 us
    pallas_call x1, Pallas kernels, on_device(): pl.pallas_call(functools.partial(inner_kernel, rows, width // BW), out_sh...  1.77 us
    pallas_call x1, Pallas kernels, on_device(): pl.pallas_call(functools.partial(pack_kernel, rows), out_shape=(edge_cols...  1.48 us
  transfers between devices with their start and end apart: 11, of which 6 were waited for; matrix products, arithmetic and copies ran while one was open for 0% of the time, Pallas kernels for 20%

profile of v2, /device:TPU:0, one launch (start us, length us, event | category | flops | bytes accessed | tf_op | source)
XLA Modules:
  0.0 42.4 jit_solution(15344860175687497841)
XLA Ops:
  0.0 1.5 %pack_edges.1 = (f32[24,128]{1,0:T(8,128)S(1)}, f32[24,128]{1,0:T(8,128)S(1)}, f32[32,256]{1,0:T(8,128)S(1)}, f32[32,256]{1,0:T(8,128)S(1)}, f32[128,128]{1,0:T(...) custom-call(f32[8,96,256]{2,1,0:T(8,128)} %fields_hbm.1, ...), custom_call_target="tpu_custom_call" | custom-call | tf_op jit(solution)/shard_map/pack_edges/pallas_call | solution.py:532
  1.5 3.0 %collective-permute-start = (f32[24,128]{1,0:T(8,128)S(1)}, f32[24,128]{1,0:T(8,128)S(1)}, u32[]{:S(2)}, u32[]{:S(2)}) collective-permute-start(f32[24,128]{1,0:T(8,128)S(1)} %get-tuple-element.32), channel_id=1, source_target_pairs={{0,1},{1,2},{2,3},{3,4},{4,5},{5,6},{6,7},{7,0},{8,9},{9,10},{10,1... | collective-permute-start | bytes 36872 | tf_op jit(solution)/shard_map/ppermute | solution.py:552
  4.5 3.1 %collective-permute-start.1 = (f32[24,128]{1,0:T(8,128)S(1)}, f32[24,128]{1,0:T(8,128)S(1)}, u32[]{:S(2)}, u32[]{:S(2)}) collective-permute-start(f32[24,128]{1,0:T(8,128)S(1)} %get-tuple-element.33), channel_id=1, source_target_pairs={{1,0},{2,1},{3,2},{4,3},{5,4},{6,5},{7,6},{0,7},{9,8},{10,9},{11,1... | collective-permute-start | bytes 36872 | tf_op jit(solution)/shard_map/ppermute | solution.py:553
  7.6 4.1 %smooth_inside.1 = (f32[192,8,128]{2,1,0:T(8,128)S(1)}, f32[8,8,256]{2,1,0:T(8,128)S(1)}, f32[32,128]{1,0:T(8,128)S(1)}, s32[16,128]{1,0:T(8,128)S(1)}, bf16[256,128,128]{2,1,0:T(8,128)(2,1)S(1)}) custom-call(f32[1768,128]{1,0:T(8,128)S(1)} %bitcast.4, f32[96,256]{1,0:T(8,128)S(1)} %get-tuple-element.29.rates, f32[96,256]{1,0:T(8,128)S(1)} %get-tuple-element.30.area, ...), custom_call_target="tpu_custom_call" | custom-call | bytes 12582912 | tf_op jit(solution)/shard_map/smooth_inside/pallas_call | solution.py:556
  11.6 0.0 collective-permute-done.west
  11.7 0.0 collective-permute-done.1.east
  11.7 0.1 join_corners.1
  11.7 0.7 %collective-permute-start.2 = (f32[24,256]{1,0:T(8,128)S(1)}, f32[24,256]{1,0:T(8,128)S(1)}, u32[]{:S(2)}, u32[]{:S(2)}) collective-permute-start(f32[24,256]{1,0:T(8,128)S(1)} %get-tuple-element.37), channel_id=1, source_target_pairs={{0,24},{8,16},{16,8},{24,0},{1,25},{9,17},{17,9},{25,1},{2,26},{10... | collective-permute-start | bytes 73736 | tf_op jit(solution)/shard_map/ppermute | solution.py:595
  12.4 1.1 %collective-permute-start.3 = (f32[24,256]{1,0:T(8,128)S(1)}, f32[24,256]{1,0:T(8,128)S(1)}, u32[]{:S(2)}, u32[]{:S(2)}) collective-permute-start(f32[24,256]{1,0:T(8,128)S(1)} %get-tuple-element.38), channel_id=1, source_target_pairs={{0,8},{8,0},{16,24},{24,16},{1,9},{9,1},{17,25},{25,17},{2,10},{10... | collective-permute-start | bytes 73736 | tf_op jit(solution)/shard_map/ppermute | solution.py:596
  13.5 1.8 %multiply_inside.1 = (f32[256,8,128]{2,1,0:T(8,128)S(1)}, f32[192,8,128]{2,1,0:T(8,128)S(1)}) custom-call(f32[24,128]{1,0:T(8,128)S(1)} %collective-permute-done.1.east, f32[24,128]{1,0:T(8,128)S(1)} %collective-permute-done.west, s32[16,128]{1,0:T(8,128)S(1)} %get-tuple-element.47.table_vmem, ...), custom_call_target="tpu_custom_call", output_to_operand_aliasing={{1}: (6, {})} | custom-call | flops 33554432 | bytes 4194304 | tf_op jit(solution)/shard_map/multiply_inside/pallas_call | solution.py:616
  15.3 0.0 collective-permute-done.2.rows_odd
  15.3 0.0 collective-permute-done.3.rows_even
  15.3 1.3 %add_edges.1 = (f32[256,8,128]{2,1,0:T(8,128)S(1)}, f32[192,8,128]{2,1,0:T(8,128)S(1)}) custom-call(f32[24,256]{1,0:T(8,128)S(1)} %collective-permute-done.2.rows_odd, f32[24,256]{1,0:T(8,128)S(1)} %collective-permute-done.3.rows_even, s32[16,128]{1,0:T(8,128)S(1)} %get-tuple-element.47.table_vmem, ...), custom_call_target="tpu_custom_call", output_to_operand_aliasing={{0}: (9, {}), {1}: (10, {})} | custom-call | tf_op jit(solution)/shard_map/add_edges/pallas_call | solution.py:629
  16.6 0.1 fusion.2
  16.7 0.1 collective-permute-start.4
  16.8 0.5 %collective-permute-start.5 = (f32[128,8,128]{2,1,0:T(8,128)S(1)}, f32[128,8,128]{2,1,0:T(8,128)S(1)}, u32[]{:S(2)}, u32[]{:S(2)}) collective-permute-start(f32[128,8,128]{2,1,0:T(8,128)S(1)} %get-tuple-element.55), channel_id=1, source_target_pairs={{0,8},{8,0},{16,24},{24,16},{1,9},{9,1},{17,25},{25,17},{2,10},{10... | collective-permute-start | bytes 1572872 | tf_op jit(solution)/shard_map/ppermute | solution.py:642
  17.3 1.2 %multiply_sent.1 = f32[128,8,128]{2,1,0:T(8,128)S(1)} custom-call(s32[16,128]{1,0:T(8,128)S(1)} %get-tuple-element.47.table_vmem, f32[192,8,128]{2,1,0:T(8,128)S(1)} %get-tuple-element.45.blocks, bf16[256,128,128]{2,1,0:T(8,128)(2,1)S(1)} %get-tuple-element.40.held), custom_call_target="tpu_custom_call" | custom-call | flops 33554432 | bytes 4194304 | tf_op jit(solution)/shard_map/multiply_sent/pallas_call | solution.py:602
  18.5 0.0 copy-start
  18.5 0.1 collective-permute-done.4
  18.7 0.1 add.48
  18.8 0.1 collective-permute-start.6
  18.8 1.2 %multiply_kept.1 = f32[128,8,128]{2,1,0:T(8,128)S(1)} custom-call(s32[16,128]{1,0:T(8,128)S(1)} %get-tuple-element.47.table_vmem, f32[192,8,128]{2,1,0:T(8,128)S(1)} %get-tuple-element.45.blocks, bf16[256,128,128]{2,1,0:T(8,128)(2,1)S(1)} %get-tuple-element.40.held), custom_call_target="tpu_custom_call" | custom-call | flops 33554432 | bytes 4194304 | tf_op jit(solution)/shard_map/multiply_kept/pallas_call | solution.py:602
  20.1 0.0 collective-permute-done.5
  20.1 7.9 %collective-permute-done.6 = f32[128,8,128]{2,1,0:T(8,128)S(1)} collective-permute-done((f32[128,8,128]{2,1,0:T(8,128)S(1)}, f32[128,8,128]{2,1,0:T(8,128)S(1)}, u32[]{:S(2)}, u32[]{:S(2)}) %collective-permute-start.6) | collective-permute-done | bytes 524320 | tf_op jit(solution)/shard_map/ppermute | solution.py:491
  28.0 0.1 slice_add_fusion.6
  28.1 0.6 %collective-permute-start.7 = (f32[32,8,128]{2,1,0:T(8,128)S(1)}, f32[32,8,128]{2,1,0:T(8,128)S(1)}, u32[]{:S(2)}, u32[]{:S(2)}) collective-permute-start(f32[32,8,128]{2,1,0:T(8,128)S(1)} %get-tuple-element.48), channel_id=1, source_target_pairs={{0,18},{1,19},{2,16},{3,17},{4,22},{5,23},{6,20},{7,21},{8,11},{9,... | collective-permute-start | bytes 393224 | tf_op jit(solution)/shard_map/ppermute | solution.py:491
  28.7 2.2 %collective-permute-start.8 = (f32[32,8,128]{2,1,0:T(8,128)S(1)}, f32[32,8,128]{2,1,0:T(8,128)S(1)}, u32[]{:S(2)}, u32[]{:S(2)}) collective-permute-start(f32[32,8,128]{2,1,0:T(8,128)S(1)} %get-tuple-element.49), channel_id=1, source_target_pairs={{0,2},{1,3},{2,0},{3,1},{4,6},{5,7},{6,4},{7,5},{8,10},{9,11},{10,... | collective-permute-start | bytes 393224 | tf_op jit(solution)/shard_map/ppermute | solution.py:491
  31.0 0.7 %collective-permute-start.9 = (f32[32,8,128]{2,1,0:T(8,128)S(1)}, f32[32,8,128]{2,1,0:T(8,128)S(1)}, u32[]{:S(2)}, u32[]{:S(2)}) collective-permute-start(f32[32,8,128]{2,1,0:T(8,128)S(1)} %get-tuple-element.50), channel_id=1, source_target_pairs={{0,16},{1,17},{2,18},{3,19},{4,20},{5,21},{6,22},{7,23},{8,9},{9,8... | collective-permute-start | bytes 393224 | tf_op jit(solution)/shard_map/ppermute | solution.py:491
  31.7 2.4 %collective-permute-done.7 = f32[32,8,128]{2,1,0:T(8,128)S(1)} collective-permute-done((f32[32,8,128]{2,1,0:T(8,128)S(1)}, f32[32,8,128]{2,1,0:T(8,128)S(1)}, u32[]{:S(2)}, u32[]{:S(2)}) %collective-permute-start.7) | collective-permute-done | bytes 131104 | tf_op jit(solution)/shard_map/ppermute | solution.py:491
  34.0 1.3 %collective-permute-done.8 = f32[32,8,128]{2,1,0:T(8,128)S(1)} collective-permute-done((f32[32,8,128]{2,1,0:T(8,128)S(1)}, f32[32,8,128]{2,1,0:T(8,128)S(1)}, u32[]{:S(2)}, u32[]{:S(2)}) %collective-permute-start.8) | collective-permute-done | bytes 131104 | tf_op jit(solution)/shard_map/ppermute | solution.py:491
  35.3 0.6 %collective-permute-done.9 = f32[32,8,128]{2,1,0:T(8,128)S(1)} collective-permute-done((f32[32,8,128]{2,1,0:T(8,128)S(1)}, f32[32,8,128]{2,1,0:T(8,128)S(1)}, u32[]{:S(2)}, u32[]{:S(2)}) %collective-permute-start.9) | collective-permute-done | bytes 131104 | tf_op jit(solution)/shard_map/ppermute | solution.py:491
  36.0 1.4 %collective-permute-start.10 = (f32[16,8,128]{2,1,0:T(8,128)S(1)}, f32[16,8,128]{2,1,0:T(8,128)S(1)}, u32[]{:S(2)}, u32[]{:S(2)}) collective-permute-start(f32[16,8,128]{2,1,0:T(8,128)S(1)} %slice_add_fusion.8), channel_id=1, source_target_pairs={{0,4},{1,5},{2,6},{3,7},{4,0},{5,1},{6,2},{7,3},{8,12},{9,13},{10,... | collective-permute-start | bytes 196616 | tf_op jit(solution)/shard_map/ppermute | solution.py:491
  37.3 4.4 %collective-permute-done.10 = f32[16,8,128]{2,1,0:T(8,128)S(1)} collective-permute-done((f32[16,8,128]{2,1,0:T(8,128)S(1)}, f32[16,8,128]{2,1,0:T(8,128)S(1)}, u32[]{:S(2)}, u32[]{:S(2)}) %collective-permute-start.10) | collective-permute-done | bytes 65568 | tf_op jit(solution)/shard_map/ppermute | solution.py:491
  41.8 0.0 copy-done
  41.8 0.7 %fusion.1 = f32[16,8,128]{2,1,0:T(8,128)} fusion(f32[16,8,128]{2,1,0:T(8,128)S(1)} %collective-permute-done.10, f32[32,8,128]{2,1,0:T(8,128)S(1)} %collective-permute-done.9, f32[32,8,128]{2,1,0:T(8,128)S(1)} %collective-permute-done.8, f32[32,8,128]{2,1,0:T(8,128)S(1)} %collective-permute-done.7, f32[32,8,128]{2,1,0:T(8,128)S(1)} %get-tuple-element.51, ...), kind=kLoop, calls=%fused_computation.13 | loop fusion | flops 81920 | bytes 401408 | tf_op jit(solution)/shard_map/div | solution.py:647
  (1 shorter events, 0.0 us)
Async XLA Ops:
  1.5 10.2 %collective-permute-start = (f32[24,128]{1,0:T(8,128)S(1)}, f32[24,128]{1,0:T(8,128)S(1)}, u32[]{:S(2)}, u32[]{:S(2)}) collective-permute-start(f32[24,128]{1,0:T(8,128)S(1)} %get-tuple-element.32), channel_id=1, source_target_pairs={{0,1},{1,2},{2,3},{3,4},{4,5},{5,6},{6,7},{7,0},{8,9},{9,10},{10,1... | collective-permute-start | bytes 36872 | tf_op jit(solution)/shard_map/ppermute | solution.py:552
  4.5 7.2 %collective-permute-start.1 = (f32[24,128]{1,0:T(8,128)S(1)}, f32[24,128]{1,0:T(8,128)S(1)}, u32[]{:S(2)}, u32[]{:S(2)}) collective-permute-start(f32[24,128]{1,0:T(8,128)S(1)} %get-tuple-element.33), channel_id=1, source_target_pairs={{1,0},{2,1},{3,2},{4,3},{5,4},{6,5},{7,6},{0,7},{9,8},{10,9},{11,1... | collective-permute-start | bytes 36872 | tf_op jit(solution)/shard_map/ppermute | solution.py:553
  11.7 3.6 %collective-permute-start.2 = (f32[24,256]{1,0:T(8,128)S(1)}, f32[24,256]{1,0:T(8,128)S(1)}, u32[]{:S(2)}, u32[]{:S(2)}) collective-permute-start(f32[24,256]{1,0:T(8,128)S(1)} %get-tuple-element.37), channel_id=1, source_target_pairs={{0,24},{8,16},{16,8},{24,0},{1,25},{9,17},{17,9},{25,1},{2,26},{10... | collective-permute-start | bytes 73736 | tf_op jit(solution)/shard_map/ppermute | solution.py:595
  12.4 2.9 %collective-permute-start.3 = (f32[24,256]{1,0:T(8,128)S(1)}, f32[24,256]{1,0:T(8,128)S(1)}, u32[]{:S(2)}, u32[]{:S(2)}) collective-permute-start(f32[24,256]{1,0:T(8,128)S(1)} %get-tuple-element.38), channel_id=1, source_target_pairs={{0,8},{8,0},{16,24},{24,16},{1,9},{9,1},{17,25},{25,17},{2,10},{10... | collective-permute-start | bytes 73736 | tf_op jit(solution)/shard_map/ppermute | solution.py:596
  16.7 2.0 %collective-permute-start.4 = (f32[128,8,128]{2,1,0:T(8,128)S(1)}, f32[128,8,128]{2,1,0:T(8,128)S(1)}, u32[]{:S(2)}, u32[]{:S(2)}) collective-permute-start(f32[128,8,128]{2,1,0:T(8,128)S(1)} %get-tuple-element.56), channel_id=1, source_target_pairs={{0,8},{8,0},{16,24},{24,16},{1,9},{9,1},{17,25},{25,17},{2,10},{10... | collective-permute-start | bytes 1572872 | tf_op jit(solution)/shard_map/ppermute | solution.py:641
  16.8 3.3 %collective-permute-start.5 = (f32[128,8,128]{2,1,0:T(8,128)S(1)}, f32[128,8,128]{2,1,0:T(8,128)S(1)}, u32[]{:S(2)}, u32[]{:S(2)}) collective-permute-start(f32[128,8,128]{2,1,0:T(8,128)S(1)} %get-tuple-element.55), channel_id=1, source_target_pairs={{0,8},{8,0},{16,24},{24,16},{1,9},{9,1},{17,25},{25,17},{2,10},{10... | collective-permute-start | bytes 1572872 | tf_op jit(solution)/shard_map/ppermute | solution.py:642
  18.5 23.2 %copy-start = (f32[16,128]{1,0:T(8,128)S(1)}, f32[16,128]{1,0:T(8,128)}, u32[]{:S(2)}) copy-start(f32[16,128]{1,0:T(8,128)} %param.15) | copy-start | bytes 24580
  18.8 9.2 %collective-permute-start.6 = (f32[128,8,128]{2,1,0:T(8,128)S(1)}, f32[128,8,128]{2,1,0:T(8,128)S(1)}, u32[]{:S(2)}, u32[]{:S(2)}) collective-permute-start(f32[128,8,128]{2,1,0:T(8,128)S(1)} %add.48), channel_id=1, source_target_pairs={{0,1},{1,0},{2,3},{3,2},{4,5},{5,4},{6,7},{7,6},{8,24},{9,25},{10,... | collective-permute-start | bytes 1572872 | tf_op jit(solution)/shard_map/ppermute | solution.py:491
  28.1 5.9 %collective-permute-start.7 = (f32[32,8,128]{2,1,0:T(8,128)S(1)}, f32[32,8,128]{2,1,0:T(8,128)S(1)}, u32[]{:S(2)}, u32[]{:S(2)}) collective-permute-start(f32[32,8,128]{2,1,0:T(8,128)S(1)} %get-tuple-element.48), channel_id=1, source_target_pairs={{0,18},{1,19},{2,16},{3,17},{4,22},{5,23},{6,20},{7,21},{8,11},{9,... | collective-permute-start | bytes 393224 | tf_op jit(solution)/shard_map/ppermute | solution.py:491
  28.7 6.6 %collective-permute-start.8 = (f32[32,8,128]{2,1,0:T(8,128)S(1)}, f32[32,8,128]{2,1,0:T(8,128)S(1)}, u32[]{:S(2)}, u32[]{:S(2)}) collective-permute-start(f32[32,8,128]{2,1,0:T(8,128)S(1)} %get-tuple-element.49), channel_id=1, source_target_pairs={{0,2},{1,3},{2,0},{3,1},{4,6},{5,7},{6,4},{7,5},{8,10},{9,11},{10,... | collective-permute-start | bytes 393224 | tf_op jit(solution)/shard_map/ppermute | solution.py:491
  31.0 5.0 %collective-permute-start.9 = (f32[32,8,128]{2,1,0:T(8,128)S(1)}, f32[32,8,128]{2,1,0:T(8,128)S(1)}, u32[]{:S(2)}, u32[]{:S(2)}) collective-permute-start(f32[32,8,128]{2,1,0:T(8,128)S(1)} %get-tuple-element.50), channel_id=1, source_target_pairs={{0,16},{1,17},{2,18},{3,19},{4,20},{5,21},{6,22},{7,23},{8,9},{9,8... | collective-permute-start | bytes 393224 | tf_op jit(solution)/shard_map/ppermute | solution.py:491
  36.0 5.8 %collective-permute-start.10 = (f32[16,8,128]{2,1,0:T(8,128)S(1)}, f32[16,8,128]{2,1,0:T(8,128)S(1)}, u32[]{:S(2)}, u32[]{:S(2)}) collective-permute-start(f32[16,8,128]{2,1,0:T(8,128)S(1)} %slice_add_fusion.8), channel_id=1, source_target_pairs={{0,4},{1,5},{2,6},{3,7},{4,0},{5,1},{6,2},{7,3},{8,12},{9,13},{10,... | collective-permute-start | bytes 196616 | tf_op jit(solution)/shard_map/ppermute | solution.py:491

commit v3 on v1

--- a/solution.py
+++ b/solution.py
@@ -254,21 +254,19 @@
             for c, tile in enumerate(tiles):
                 blocks[third * columns + h * 8 + c] = tile
         second = jnp.clip(i - 2, 0, groups - 1)
-        out = []
+        v = once[second * BH]
         for j in range(BH):
             y = second * BH + j
-            smooth, below_2 = step(once[y], once[y + 1], y, below_2)
-            out.append(rounded(jnp.broadcast_to(area[pl.ds(y, 1), :], smooth.shape) * smooth))
-        fresh = []
+            v_n = once[y + 1]
+            smooth, below_2 = step(v, v_n, y, below_2)
+            scaled[j] = rounded(jnp.broadcast_to(area[pl.ds(y, 1), :], smooth.shape) * smooth)
+            v = v_n
         first = jnp.minimum(i, groups - 1) * BH
-        lines = [row_of(first + j) for j in range(BH + 1)]
+        v = row_of(first)
         for j in range(BH):
-            smooth, below_1 = step(lines[j], lines[j + 1], first + j, below_1)
-            fresh.append(smooth)
-        for j in range(BH):
-            scaled[j] = out[j]
-        for j in range(BH):
-            once[i * BH + j] = fresh[j]
+            v_n = row_of(first + j + 1)
+            once[i * BH + j], below_1 = step(v, v_n, first + j, below_1)
+            v = v_n
         return below_1, below_2
 
     zero = jnp.zeros((count, width), jnp.float32)

time: 42.3 us -> 41.4 us (0.979)
  waiting for transfers between devices: 16.2 us -> 14.6 us
  Pallas kernels: 11.1 us -> 11.7 us
    ppermute x5, waiting for transfers between devices: 16.1 us -> 14.6 us  [swap_parts(): lax.ppermute(part, ('ty', 'tx'), [(i, partner(i, q)) for i in range(n_ty...]
  transfers between devices with their start and end apart: 11 -> 11, of which waited for: 5 -> 5; matrix products, arithmetic and copies ran while one was open for 0% -> 0% of each run, Pallas kernels for 20% -> 21%
where the time goes in v3:
time: 41.4 us; the launch traced here: 41.3 us
  waiting for transfers between devices  14.6 us (35%)
  starting transfers between devices  13.9 us (34%)
  Pallas kernels  11.7 us (28%)
  other arithmetic  0.87 us (2%)
    ppermute x5, waiting for transfers between devices, swap_parts(): lax.ppermute(part, ('ty', 'tx'), [(i, partner(i, q)) for i in range(n_ty...  14.6 us
    ppermute x5, starting transfers between devices, swap_parts(): lax.ppermute(part, ('ty', 'tx'), [(i, partner(i, q)) for i in range(n_ty...  5.44 us
    pallas_call x1, Pallas kernels, on_device(): pl.pallas_call(functools.partial(smooth_kernel, rows, sizes), out_shape=(...  4.05 us
    ppermute x1, starting transfers between devices, on_device(): lax.ppermute(west_cols, 'tx', [((i + 1) % n_tx, i) for i in range(n_tx)])  3.1 us
    pallas_call x2, Pallas kernels, sums_of(): pl.pallas_call(functools.partial(sum_kernel, kind, first_row), out_shape=...  3.01 us
    ppermute x1, starting transfers between devices, on_device(): lax.ppermute(east_cols, 'tx', [(i, (i + 1) % n_tx) for i in range(n_tx)])  2.99 us
    pallas_call x1, Pallas kernels, on_device(): pl.pallas_call(functools.partial(inner_kernel, rows, width // BW), out_sh...  1.77 us
    pallas_call x1, Pallas kernels, on_device(): pl.pallas_call(functools.partial(pack_kernel, rows), out_shape=(edge_cols...  1.48 us
  transfers between devices with their start and end apart: 11, of which 5 were waited for; matrix products, arithmetic and copies ran while one was open for 0% of the time, Pallas kernels for 21%

profile of v3, /device:TPU:0, one launch (start us, length us, event | category | flops | bytes accessed | tf_op | source)
XLA Modules:
  0.0 41.3 jit_solution(9867724428072652768)
XLA Ops:
  0.0 1.5 %pack_edges.1 = (f32[24,128]{1,0:T(8,128)S(1)}, f32[24,128]{1,0:T(8,128)S(1)}, f32[32,256]{1,0:T(8,128)S(1)}, f32[32,256]{1,0:T(8,128)S(1)}, f32[128,128]{1,0:T(...) custom-call(f32[8,96,256]{2,1,0:T(8,128)} %fields_hbm.1, ...), custom_call_target="tpu_custom_call" | custom-call | tf_op jit(solution)/shard_map/pack_edges/pallas_call | solution.py:530
  1.5 3.0 %collective-permute-start = (f32[24,128]{1,0:T(8,128)S(1)}, f32[24,128]{1,0:T(8,128)S(1)}, u32[]{:S(2)}, u32[]{:S(2)}) collective-permute-start(f32[24,128]{1,0:T(8,128)S(1)} %get-tuple-element.32), channel_id=1, source_target_pairs={{0,1},{1,2},{2,3},{3,4},{4,5},{5,6},{6,7},{7,0},{8,9},{9,10},{10,1... | collective-permute-start | bytes 36872 | tf_op jit(solution)/shard_map/ppermute | solution.py:550
  4.5 3.1 %collective-permute-start.1 = (f32[24,128]{1,0:T(8,128)S(1)}, f32[24,128]{1,0:T(8,128)S(1)}, u32[]{:S(2)}, u32[]{:S(2)}) collective-permute-start(f32[24,128]{1,0:T(8,128)S(1)} %get-tuple-element.33), channel_id=1, source_target_pairs={{1,0},{2,1},{3,2},{4,3},{5,4},{6,5},{7,6},{0,7},{9,8},{10,9},{11,1... | collective-permute-start | bytes 36872 | tf_op jit(solution)/shard_map/ppermute | solution.py:551
  7.6 4.1 %smooth_inside.1 = (f32[192,8,128]{2,1,0:T(8,128)S(1)}, f32[8,8,256]{2,1,0:T(8,128)S(1)}, f32[32,128]{1,0:T(8,128)S(1)}, s32[16,128]{1,0:T(8,128)S(1)}, bf16[256,128,128]{2,1,0:T(8,128)(2,1)S(1)}) custom-call(f32[1768,128]{1,0:T(8,128)S(1)} %bitcast.4, f32[96,256]{1,0:T(8,128)S(1)} %get-tuple-element.29.rates, f32[96,256]{1,0:T(8,128)S(1)} %get-tuple-element.30.area, ...), custom_call_target="tpu_custom_call" | custom-call | bytes 12582912 | tf_op jit(solution)/shard_map/smooth_inside/pallas_call | solution.py:554
  11.6 0.0 collective-permute-done.west
  11.7 0.0 collective-permute-done.1.east
  11.7 0.1 join_corners.1
  11.7 0.7 %collective-permute-start.2 = (f32[24,256]{1,0:T(8,128)S(1)}, f32[24,256]{1,0:T(8,128)S(1)}, u32[]{:S(2)}, u32[]{:S(2)}) collective-permute-start(f32[24,256]{1,0:T(8,128)S(1)} %get-tuple-element.37), channel_id=1, source_target_pairs={{0,24},{8,16},{16,8},{24,0},{1,25},{9,17},{17,9},{25,1},{2,26},{10... | collective-permute-start | bytes 73736 | tf_op jit(solution)/shard_map/ppermute | solution.py:593
  12.4 1.1 %collective-permute-start.3 = (f32[24,256]{1,0:T(8,128)S(1)}, f32[24,256]{1,0:T(8,128)S(1)}, u32[]{:S(2)}, u32[]{:S(2)}) collective-permute-start(f32[24,256]{1,0:T(8,128)S(1)} %get-tuple-element.38), channel_id=1, source_target_pairs={{0,8},{8,0},{16,24},{24,16},{1,9},{9,1},{17,25},{25,17},{2,10},{10... | collective-permute-start | bytes 73736 | tf_op jit(solution)/shard_map/ppermute | solution.py:594
  13.5 1.8 %multiply_inside.1 = (f32[256,8,128]{2,1,0:T(8,128)S(1)}, f32[192,8,128]{2,1,0:T(8,128)S(1)}) custom-call(f32[24,128]{1,0:T(8,128)S(1)} %collective-permute-done.1.east, f32[24,128]{1,0:T(8,128)S(1)} %collective-permute-done.west, s32[16,128]{1,0:T(8,128)S(1)} %get-tuple-element.47.table_vmem, ...), custom_call_target="tpu_custom_call", output_to_operand_aliasing={{1}: (6, {})} | custom-call | flops 33554432 | bytes 4194304 | tf_op jit(solution)/shard_map/multiply_inside/pallas_call | solution.py:614
  15.3 0.0 collective-permute-done.2.rows_odd
  15.3 0.0 collective-permute-done.3.rows_even
  15.3 1.3 %add_edges.1 = (f32[256,8,128]{2,1,0:T(8,128)S(1)}, f32[192,8,128]{2,1,0:T(8,128)S(1)}) custom-call(f32[24,256]{1,0:T(8,128)S(1)} %collective-permute-done.2.rows_odd, f32[24,256]{1,0:T(8,128)S(1)} %collective-permute-done.3.rows_even, s32[16,128]{1,0:T(8,128)S(1)} %get-tuple-element.47.table_vmem, ...), custom_call_target="tpu_custom_call", output_to_operand_aliasing={{0}: (9, {}), {1}: (10, {})} | custom-call | tf_op jit(solution)/shard_map/add_edges/pallas_call | solution.py:627
  16.6 0.1 fusion.2
  16.7 0.1 collective-permute-start.4
  16.8 0.5 %collective-permute-start.5 = (f32[128,8,128]{2,1,0:T(8,128)S(1)}, f32[128,8,128]{2,1,0:T(8,128)S(1)}, u32[]{:S(2)}, u32[]{:S(2)}) collective-permute-start(f32[128,8,128]{2,1,0:T(8,128)S(1)} %get-tuple-element.55), channel_id=1, source_target_pairs={{0,8},{8,0},{16,24},{24,16},{1,9},{9,1},{17,25},{25,17},{2,10},{10... | collective-permute-start | bytes 1572872 | tf_op jit(solution)/shard_map/ppermute | solution.py:640
  17.3 1.5 %multiply_sent.1 = f32[128,8,128]{2,1,0:T(8,128)S(1)} custom-call(s32[16,128]{1,0:T(8,128)S(1)} %get-tuple-element.47.table_vmem, f32[192,8,128]{2,1,0:T(8,128)S(1)} %get-tuple-element.45.blocks, bf16[256,128,128]{2,1,0:T(8,128)(2,1)S(1)} %get-tuple-element.40.held), custom_call_target="tpu_custom_call" | custom-call | flops 33554432 | bytes 4194304 | tf_op jit(solution)/shard_map/multiply_sent/pallas_call | solution.py:600
  18.8 0.0 copy-start
  18.8 0.0 collective-permute-done.4
  18.8 0.1 add.48
  18.9 0.1 collective-permute-start.6
  19.0 1.5 %multiply_kept.1 = f32[128,8,128]{2,1,0:T(8,128)S(1)} custom-call(s32[16,128]{1,0:T(8,128)S(1)} %get-tuple-element.47.table_vmem, f32[192,8,128]{2,1,0:T(8,128)S(1)} %get-tuple-element.45.blocks, bf16[256,128,128]{2,1,0:T(8,128)(2,1)S(1)} %get-tuple-element.40.held), custom_call_target="tpu_custom_call" | custom-call | flops 33554432 | bytes 4194304 | tf_op jit(solution)/shard_map/multiply_kept/pallas_call | solution.py:600
  20.5 0.0 collective-permute-done.5
  20.5 7.6 %collective-permute-done.6 = f32[128,8,128]{2,1,0:T(8,128)S(1)} collective-permute-done((f32[128,8,128]{2,1,0:T(8,128)S(1)}, f32[128,8,128]{2,1,0:T(8,128)S(1)}, u32[]{:S(2)}, u32[]{:S(2)}) %collective-permute-start.6) | collective-permute-done | bytes 524320 | tf_op jit(solution)/shard_map/ppermute | solution.py:489
  28.2 0.1 slice_add_fusion.6
  28.3 0.6 %collective-permute-start.7 = (f32[32,8,128]{2,1,0:T(8,128)S(1)}, f32[32,8,128]{2,1,0:T(8,128)S(1)}, u32[]{:S(2)}, u32[]{:S(2)}) collective-permute-start(f32[32,8,128]{2,1,0:T(8,128)S(1)} %get-tuple-element.48), channel_id=1, source_target_pairs={{0,18},{1,19},{2,16},{3,17},{4,22},{5,23},{6,20},{7,21},{8,11},{9,... | collective-permute-start | bytes 393224 | tf_op jit(solution)/shard_map/ppermute | solution.py:489
  28.9 0.7 %collective-permute-start.8 = (f32[32,8,128]{2,1,0:T(8,128)S(1)}, f32[32,8,128]{2,1,0:T(8,128)S(1)}, u32[]{:S(2)}, u32[]{:S(2)}) collective-permute-start(f32[32,8,128]{2,1,0:T(8,128)S(1)} %get-tuple-element.49), channel_id=1, source_target_pairs={{0,16},{1,17},{2,18},{3,19},{4,20},{5,21},{6,22},{7,23},{8,10},{9,... | collective-permute-start | bytes 393224 | tf_op jit(solution)/shard_map/ppermute | solution.py:489
  29.6 2.2 %collective-permute-start.9 = (f32[32,8,128]{2,1,0:T(8,128)S(1)}, f32[32,8,128]{2,1,0:T(8,128)S(1)}, u32[]{:S(2)}, u32[]{:S(2)}) collective-permute-start(f32[32,8,128]{2,1,0:T(8,128)S(1)} %get-tuple-element.50), channel_id=1, source_target_pairs={{0,2},{1,3},{2,0},{3,1},{4,6},{5,7},{6,4},{7,5},{8,9},{9,8},{10,11... | collective-permute-start | bytes 393224 | tf_op jit(solution)/shard_map/ppermute | solution.py:489
  31.8 2.5 %collective-permute-done.7 = f32[32,8,128]{2,1,0:T(8,128)S(1)} collective-permute-done((f32[32,8,128]{2,1,0:T(8,128)S(1)}, f32[32,8,128]{2,1,0:T(8,128)S(1)}, u32[]{:S(2)}, u32[]{:S(2)}) %collective-permute-start.7) | collective-permute-done | bytes 131104 | tf_op jit(solution)/shard_map/ppermute | solution.py:489
  34.3 1.0 %collective-permute-done.8 = f32[32,8,128]{2,1,0:T(8,128)S(1)} collective-permute-done((f32[32,8,128]{2,1,0:T(8,128)S(1)}, f32[32,8,128]{2,1,0:T(8,128)S(1)}, u32[]{:S(2)}, u32[]{:S(2)}) %collective-permute-start.8) | collective-permute-done | bytes 131104 | tf_op jit(solution)/shard_map/ppermute | solution.py:489
  35.3 0.1 collective-permute-done.9
  35.4 1.8 %collective-permute-start.10 = (f32[16,8,128]{2,1,0:T(8,128)S(1)}, f32[16,8,128]{2,1,0:T(8,128)S(1)}, u32[]{:S(2)}, u32[]{:S(2)}) collective-permute-start(f32[16,8,128]{2,1,0:T(8,128)S(1)} %slice_add_fusion.8), channel_id=1, source_target_pairs={{0,4},{1,5},{2,6},{3,7},{4,0},{5,1},{6,2},{7,3},{8,12},{9,13},{10,... | collective-permute-start | bytes 196616 | tf_op jit(solution)/shard_map/ppermute | solution.py:489
  37.2 3.4 %collective-permute-done.10 = f32[16,8,128]{2,1,0:T(8,128)S(1)} collective-permute-done((f32[16,8,128]{2,1,0:T(8,128)S(1)}, f32[16,8,128]{2,1,0:T(8,128)S(1)}, u32[]{:S(2)}, u32[]{:S(2)}) %collective-permute-start.10) | collective-permute-done | bytes 65568 | tf_op jit(solution)/shard_map/ppermute | solution.py:489
  40.6 0.0 copy-done
  40.6 0.7 %fusion.1 = f32[16,8,128]{2,1,0:T(8,128)} fusion(f32[16,8,128]{2,1,0:T(8,128)S(1)} %collective-permute-done.10, f32[32,8,128]{2,1,0:T(8,128)S(1)} %collective-permute-done.9, f32[32,8,128]{2,1,0:T(8,128)S(1)} %collective-permute-done.8, f32[32,8,128]{2,1,0:T(8,128)S(1)} %collective-permute-done.7, f32[32,8,128]{2,1,0:T(8,128)S(1)} %get-tuple-element.51, ...), kind=kLoop, calls=%fused_computation.13 | loop fusion | flops 81920 | bytes 401408 | tf_op jit(solution)/shard_map/div | solution.py:645
  (1 shorter events, 0.0 us)
Async XLA Ops:
  1.5 10.2 %collective-permute-start = (f32[24,128]{1,0:T(8,128)S(1)}, f32[24,128]{1,0:T(8,128)S(1)}, u32[]{:S(2)}, u32[]{:S(2)}) collective-permute-start(f32[24,128]{1,0:T(8,128)S(1)} %get-tuple-element.32), channel_id=1, source_target_pairs={{0,1},{1,2},{2,3},{3,4},{4,5},{5,6},{6,7},{7,0},{8,9},{9,10},{10,1... | collective-permute-start | bytes 36872 | tf_op jit(solution)/shard_map/ppermute | solution.py:550
  4.5 7.2 %collective-permute-start.1 = (f32[24,128]{1,0:T(8,128)S(1)}, f32[24,128]{1,0:T(8,128)S(1)}, u32[]{:S(2)}, u32[]{:S(2)}) collective-permute-start(f32[24,128]{1,0:T(8,128)S(1)} %get-tuple-element.33), channel_id=1, source_target_pairs={{1,0},{2,1},{3,2},{4,3},{5,4},{6,5},{7,6},{0,7},{9,8},{10,9},{11,1... | collective-permute-start | bytes 36872 | tf_op jit(solution)/shard_map/ppermute | solution.py:551
  11.7 3.6 %collective-permute-start.2 = (f32[24,256]{1,0:T(8,128)S(1)}, f32[24,256]{1,0:T(8,128)S(1)}, u32[]{:S(2)}, u32[]{:S(2)}) collective-permute-start(f32[24,256]{1,0:T(8,128)S(1)} %get-tuple-element.37), channel_id=1, source_target_pairs={{0,24},{8,16},{16,8},{24,0},{1,25},{9,17},{17,9},{25,1},{2,26},{10... | collective-permute-start | bytes 73736 | tf_op jit(solution)/shard_map/ppermute | solution.py:593
  12.4 2.9 %collective-permute-start.3 = (f32[24,256]{1,0:T(8,128)S(1)}, f32[24,256]{1,0:T(8,128)S(1)}, u32[]{:S(2)}, u32[]{:S(2)}) collective-permute-start(f32[24,256]{1,0:T(8,128)S(1)} %get-tuple-element.38), channel_id=1, source_target_pairs={{0,8},{8,0},{16,24},{24,16},{1,9},{9,1},{17,25},{25,17},{2,10},{10... | collective-permute-start | bytes 73736 | tf_op jit(solution)/shard_map/ppermute | solution.py:594
  16.7 2.1 %collective-permute-start.4 = (f32[128,8,128]{2,1,0:T(8,128)S(1)}, f32[128,8,128]{2,1,0:T(8,128)S(1)}, u32[]{:S(2)}, u32[]{:S(2)}) collective-permute-start(f32[128,8,128]{2,1,0:T(8,128)S(1)} %get-tuple-element.56), channel_id=1, source_target_pairs={{0,8},{8,0},{16,24},{24,16},{1,9},{9,1},{17,25},{25,17},{2,10},{10... | collective-permute-start | bytes 1572872 | tf_op jit(solution)/shard_map/ppermute | solution.py:639
  16.8 3.7 %collective-permute-start.5 = (f32[128,8,128]{2,1,0:T(8,128)S(1)}, f32[128,8,128]{2,1,0:T(8,128)S(1)}, u32[]{:S(2)}, u32[]{:S(2)}) collective-permute-start(f32[128,8,128]{2,1,0:T(8,128)S(1)} %get-tuple-element.55), channel_id=1, source_target_pairs={{0,8},{8,0},{16,24},{24,16},{1,9},{9,1},{17,25},{25,17},{2,10},{10... | collective-permute-start | bytes 1572872 | tf_op jit(solution)/shard_map/ppermute | solution.py:640
  18.8 21.8 %copy-start = (f32[16,128]{1,0:T(8,128)S(1)}, f32[16,128]{1,0:T(8,128)}, u32[]{:S(2)}) copy-start(f32[16,128]{1,0:T(8,128)} %param.15) | copy-start | bytes 24580
  18.9 9.2 %collective-permute-start.6 = (f32[128,8,128]{2,1,0:T(8,128)S(1)}, f32[128,8,128]{2,1,0:T(8,128)S(1)}, u32[]{:S(2)}, u32[]{:S(2)}) collective-permute-start(f32[128,8,128]{2,1,0:T(8,128)S(1)} %add.48), channel_id=1, source_target_pairs={{0,1},{1,0},{2,3},{3,2},{4,5},{5,4},{6,7},{7,6},{8,24},{9,25},{10,... | collective-permute-start | bytes 1572872 | tf_op jit(solution)/shard_map/ppermute | solution.py:489
  28.3 6.0 %collective-permute-start.7 = (f32[32,8,128]{2,1,0:T(8,128)S(1)}, f32[32,8,128]{2,1,0:T(8,128)S(1)}, u32[]{:S(2)}, u32[]{:S(2)}) collective-permute-start(f32[32,8,128]{2,1,0:T(8,128)S(1)} %get-tuple-element.48), channel_id=1, source_target_pairs={{0,18},{1,19},{2,16},{3,17},{4,22},{5,23},{6,20},{7,21},{8,11},{9,... | collective-permute-start | bytes 393224 | tf_op jit(solution)/shard_map/ppermute | solution.py:489
  28.9 6.4 %collective-permute-start.8 = (f32[32,8,128]{2,1,0:T(8,128)S(1)}, f32[32,8,128]{2,1,0:T(8,128)S(1)}, u32[]{:S(2)}, u32[]{:S(2)}) collective-permute-start(f32[32,8,128]{2,1,0:T(8,128)S(1)} %get-tuple-element.49), channel_id=1, source_target_pairs={{0,16},{1,17},{2,18},{3,19},{4,20},{5,21},{6,22},{7,23},{8,10},{9,... | collective-permute-start | bytes 393224 | tf_op jit(solution)/shard_map/ppermute | solution.py:489
  29.6 5.8 %collective-permute-start.9 = (f32[32,8,128]{2,1,0:T(8,128)S(1)}, f32[32,8,128]{2,1,0:T(8,128)S(1)}, u32[]{:S(2)}, u32[]{:S(2)}) collective-permute-start(f32[32,8,128]{2,1,0:T(8,128)S(1)} %get-tuple-element.50), channel_id=1, source_target_pairs={{0,2},{1,3},{2,0},{3,1},{4,6},{5,7},{6,4},{7,5},{8,9},{9,8},{10,11... | collective-permute-start | bytes 393224 | tf_op jit(solution)/shard_map/ppermute | solution.py:489
  35.4 5.2 %collective-permute-start.10 = (f32[16,8,128]{2,1,0:T(8,128)S(1)}, f32[16,8,128]{2,1,0:T(8,128)S(1)}, u32[]{:S(2)}, u32[]{:S(2)}) collective-permute-start(f32[16,8,128]{2,1,0:T(8,128)S(1)} %slice_add_fusion.8), channel_id=1, source_target_pairs={{0,4},{1,5},{2,6},{3,7},{4,0},{5,1},{6,2},{7,3},{8,12},{9,13},{10,... | collective-permute-start | bytes 196616 | tf_op jit(solution)/shard_map/ppermute | solution.py:489
